TPU v7x, 32 devices: a whole 2x2x4 slice. The times are simulated.
32 devices in a mesh: gx: 4 (over y, core), gy: 8 (over z, x).
Axes of the slice: x: 2, y: 2, z: 4, core: 2. Of those that a mesh axis runs over, the one named last changes fastest.
Arguments:
- model_state: float32 [3, 8, 1536, 1024], P(None, None, 'gx', 'gy'), may hold values from -6 to 6
- obs_val: float32 [4096, 384], P(('gx', 'gy')), may hold values from -6 to 6
- obs_owner: int32 [4096, 1], P(('gx', 'gy')), may hold values from 0 to 7; in each aligned block of 128 rows (0 to 127, 128 to 255, ...) at most 32 rows name the same one
- obs_x: int32 [4096], P(('gx', 'gy')), may hold values from 0 to 1535
- obs_y: int32 [4096], P(('gx', 'gy')), may hold values from 0 to 127
- cressman: float32 [1536, 1536], P(None, 'gx'), as said below
- vertical: float32 [3, 8, 128], replicated, may hold values from -2 to 2
Outputs:
- new_state: float32 [3, 8, 1536, 1024], P(None, None, 'gx', 'gy')
Inputs may be any that keep to these rules, and one draw needn't show every extreme that they name: `obs_owner`: among the rows of one device, at most 32 name one column; in every draw some device's rows name some column exactly 32 times. `cressman`: entries are positive.
All inputs are finite; a program needn't handle non-finite values.
Results may differ from a plain program's by a relative error of at most 0.0001.
Values sent between devices are 32-bit elements; how exact they have to be, the bound alone decides.
No kernel may reach another device: no remote copies, remote signals or barrier semaphores. Data moves between devices by JAX's collectives and lax.ppermute only.
A program may use at most 128 MiB of HBM per device.

v0:
```python
import functools

import jax
import jax.numpy as jnp
from jax import lax
from jax.experimental import pallas as pl
from jax.experimental.pallas import tpu as pltpu
from jax.sharding import PartitionSpec as P

advect_coef = 0.5
diffuse_h = 0.2
diffuse_z = 0.1
time_step = 0.5
nudge_gain = 1.0
spread_gain = 0.125

LANES = 128
WORDS = 32
LANE_STEP = 32
YB = 16
RB = 256
VMEM_LIMIT = 48 * 1024 * 1024

HIGHEST = lax.Precision.HIGHEST
NT = (((1,), (1,)), ((), ()))
NN = (((1,), (0,)), ((), ()))
VMEM = pl.BlockSpec(memory_space=pltpu.VMEM)
ANY = pl.BlockSpec(memory_space=pl.ANY)
SMEM = pl.BlockSpec(memory_space=pltpu.SMEM)


def dot(a, b, dims=NN, precision=None):
    return lax.dot_general(a, b, dims, precision=precision, preferred_element_type=jnp.float32)


def split2(value):
    high = value.astype(jnp.bfloat16)
    low = (value - high.astype(jnp.float32)).astype(jnp.bfloat16)
    return high, low


def iota(shape, axis):
    return lax.broadcasted_iota(jnp.int32, shape, axis)


def pack_kernel(count_y, cap, owner_ref, x_ref, y_ref, obs_ref, vert_ref, msg_ref, gram_ref):
    records = x_ref.shape[1]
    kinds = vert_ref.shape[0]
    levels = kinds // 3
    vert = vert_ref[...]
    terms = []
    for v in range(3):
        obs = obs_ref[:, v * LANES : (v + 1) * LANES]
        terms.append(dot(vert[v * levels : (v + 1) * levels], obs, NT, HIGHEST) * spread_gain)
    row = iota((8, records), 0)
    x_row = jnp.broadcast_to(x_ref[...].astype(jnp.float32), (8, records))
    y_row = jnp.broadcast_to(y_ref[...].astype(jnp.float32) - float(LANES), (8, records))
    head = jnp.where(row == 0, x_row, jnp.where(row == 1, y_row, 0.0))
    payload = jnp.concatenate([head] + terms, axis=0)

    owner = owner_ref[...].astype(jnp.float32)
    owner_lanes = jnp.broadcast_to(owner, (records, records))
    owner_rows = jnp.transpose(owner_lanes)
    earlier = iota((records, records), 0) < iota((records, records), 1)
    same = jnp.where((owner_lanes == owner_rows) & earlier, 1.0, 0.0)
    rank = jnp.sum(same, axis=0, keepdims=True)
    slot = owner * float(cap) + rank
    places = count_y * cap
    pick = jnp.where(iota((places, records), 0).astype(jnp.float32) == slot, 1.0, 0.0)
    out = dot(payload, pick, NT, HIGHEST)

    lane = iota((8, LANES), 1)
    for c in range(count_y):
        chunk = (c * cap) // LANES
        offset = (c * cap) % LANES
        block = jnp.zeros((8, LANES), jnp.float32)
        for j in range(WORDS // 8):
            part = out[8 * j : 8 * j + 8, chunk * LANES : (chunk + 1) * LANES]
            shift = (LANE_STEP * j - offset) % LANES
            if shift:
                part = pltpu.roll(part, shift, 1)
            inside = (lane >= LANE_STEP * j) & (lane < LANE_STEP * j + cap)
            block = jnp.where(inside, part, block)
        for g in range(msg_ref.shape[0] // count_y):
            msg_ref[g * count_y + c] = block

    gram = dot(vert, vert, NT, HIGHEST) * spread_gain
    alike = (iota((kinds, kinds), 0) // levels) == (iota((kinds, kinds), 1) // levels)
    gram_ref[...] = jnp.where(alike, gram, 0.0)


def turn_kernel(planes, state_ref, cress_ref, hi_ref, lo_ref, ct_hi_ref, ct_lo_ref, first_y_ref, last_y_ref, first_x_ref, last_x_ref):
    step = pl.program_id(0)
    for p in range(planes):
        k = step * planes + p
        plane = state_ref[p]
        turned = jnp.transpose(plane)
        high, low = split2(turned)
        hi_ref[p] = high
        lo_ref[p] = low
        first_y_ref[pl.ds(k, 1), :] = turned[0:1]
        last_y_ref[pl.ds(k, 1), :] = turned[turned.shape[0] - 1 :]
        first_x_ref[pl.ds(k, 1), :] = plane[0:1]
        last_x_ref[pl.ds(k, 1), :] = plane[plane.shape[0] - 1 :]
    high, low = split2(jnp.transpose(cress_ref[...]))
    ct_hi_ref[...] = high
    ct_lo_ref[...] = low


def unpack(recv_ref, cap, j):
    devices = recv_ref.shape[0]
    per = LANES // cap
    lane = iota((8, LANES), 1)
    chunks = []
    for q in range(devices // per):
        block = jnp.zeros((8, LANES), jnp.float32)
        for t in range(per):
            part = recv_ref[q * per + t]
            shift = (cap * t - LANE_STEP * j) % LANES
            if shift:
                part = pltpu.roll(part, shift, 1)
            inside = (lane >= cap * t) & (lane < cap * t + cap)
            block = jnp.where(inside, part, block)
        chunks.append(block)
    return chunks


def edge_place(slots, k, side):
    per = slots // LANES
    rows = -(-24 // per)
    return 25 + side * rows + k // per, (k % per) * LANES


def sums_kernel(
    cap, tile_y, recv_ref, first_x_ref, last_x_ref, mt_hi_hbm, mt_lo_hbm, ct_hi_hbm, ct_lo_hbm,
    msg_ref, wt_hi_ref, wt_lo_ref, ys_ref, terms_ref, bounds_ref,
    mt_hi, mt_lo, ct_hi, ct_lo, rank_ref, acc_ref, sems,
):
    copies = [
        pltpu.make_async_copy(src, dst, sems.at[i])
        for i, (src, dst) in enumerate(
            ((ct_hi_hbm, ct_hi), (ct_lo_hbm, ct_lo), (mt_hi_hbm, mt_hi), (mt_lo_hbm, mt_lo))
        )
    ]
    for copy in copies:
        copy.start()
    slots = recv_ref.shape[0] * cap
    chunks = slots // LANES
    kinds, _, tile_x = mt_hi.shape
    width = ct_hi.shape[1]

    groups = [unpack(recv_ref, cap, j) for j in range(WORDS // 8)]
    keys = []
    for c in range(chunks):
        place = (iota((1, LANES), 1) + c * LANES).astype(jnp.float32)
        keys.append((groups[0][c][1:2] + float(tile_y)) * float(slots) + place)
    counts = [jnp.zeros((8, LANES), jnp.float32) for _ in range(chunks)]
    for c in range(chunks):
        column = jnp.transpose(jnp.broadcast_to(keys[c], (LANES, LANES)))
        for d in range(chunks):
            less = jnp.where(column < keys[d], 1.0, 0.0)
            counts[d] = counts[d] + jnp.sum(less.reshape(LANES // 8, 8, LANES), axis=0)
    rank = jnp.concatenate([jnp.sum(count, axis=0, keepdims=True) for count in counts], axis=1)

    rows = []
    head = jnp.concatenate(groups[0], axis=1)
    x_high = jnp.floor(head[0:1] * 0.125)
    row = iota((8, slots), 0)
    top = jnp.where(
        row == 0,
        jnp.broadcast_to(x_high, (8, slots)),
        jnp.where(
            row == 1,
            jnp.broadcast_to(head[0:1] - 8.0 * x_high, (8, slots)),
            jnp.where(row == 2, jnp.broadcast_to(head[1:2] + float(tile_y), (8, slots)), 0.0),
        ),
    )
    words = jnp.concatenate([jnp.concatenate(group, axis=1) for group in groups[1:]], axis=0)
    high = words.astype(jnp.bfloat16).astype(jnp.float32)
    middle = (words - high).astype(jnp.bfloat16).astype(jnp.float32)
    low = words - high - middle
    table = jnp.concatenate([top, high, middle, low], axis=0).astype(jnp.bfloat16)

    for copy in copies[:2]:
        copy.wait()
    blocks = slots // RB
    for j in range(blocks):
        lanes = slice(j * RB, (j + 1) * RB)
        place = (iota((RB, slots), 0) + j * RB).astype(jnp.float32)
        pick = jnp.where(place == rank, 1.0, 0.0).astype(jnp.bfloat16)
        ordered = dot(table, pick, NT)
        xs = ordered[0:1] * 8.0 + ordered[1:2]
        ys = ordered[2:3]
        ys_ref[:, lanes] = jnp.broadcast_to(ys, (8, RB))
        terms_ref[:, lanes] = ordered[8:32] + ordered[32:56] + ordered[56:80]
        hot = jnp.where(iota((width, RB), 0).astype(jnp.float32) == xs, 1.0, 0.0)
        hot = hot.astype(jnp.bfloat16)
        wt_hi_ref[:, lanes] = dot(ct_hi[...], hot).astype(jnp.bfloat16)
        wt_lo_ref[:, lanes] = dot(ct_lo[...], hot).astype(jnp.bfloat16)
        least = jnp.min(ys).astype(jnp.int32)
        most = jnp.minimum(jnp.max(ys).astype(jnp.int32), tile_y - 1)
        bounds_ref[2 * j] = least // YB
        bounds_ref[2 * j + 1] = most // YB + 1

    for copy in copies[2:]:
        copy.wait()
    ones = jnp.ones((8, tile_x), jnp.bfloat16)
    for j in range(blocks):
        lanes = slice(j * RB, (j + 1) * RB)
        acc_ref[...] = jnp.zeros_like(acc_ref)

        def add_pair(b, carry, lanes=lanes):
            start = pl.multiple_of(b * YB, YB)
            a_hi = mt_hi[:, pl.ds(start, YB), :].reshape(kinds * YB, tile_x)
            a_lo = mt_lo[:, pl.ds(start, YB), :].reshape(kinds * YB, tile_x)
            w_hi, w_lo = wt_hi_ref[:, lanes], wt_lo_ref[:, lanes]
            part = dot(a_hi, w_hi) + dot(a_hi, w_lo) + dot(a_lo, w_hi)
            named = (iota((YB, RB), 0) + start).astype(jnp.float32) == ys_ref[0:1, lanes]
            kept = jnp.where(named[None], part.reshape(kinds, YB, RB), 0.0)
            acc_ref[...] += kept[:, :8] + kept[:, 8:]
            return carry

        lax.fori_loop(bounds_ref[2 * j], bounds_ref[2 * j + 1], add_pair, 0)
        msg_ref[0:kinds, lanes] = jnp.sum(acc_ref[...], axis=1)
        total = dot(ones, wt_hi_ref[:, lanes]) + dot(ones, wt_lo_ref[:, lanes])
        msg_ref[kinds : kinds + 1, lanes] = total[0:1]
    msg_ref[kinds + 1 :, :] = jnp.zeros((WORDS - kinds - 1, slots), jnp.float32)
    for side, edge_ref in enumerate((first_x_ref, last_x_ref)):
        for k in range(kinds):
            r, at = edge_place(slots, k, side)
            msg_ref[r : r + 1, at : at + LANES] = edge_ref[k : k + 1, :]


def stencil_kernel(state_hbm, out_hbm, state, out, in_sems, out_sems):
    fields, levels, tile_x, tile_y = state.shape
    reads = [
        pltpu.make_async_copy(state_hbm.at[:, z], state.at[:, z], in_sems.at[z])
        for z in range(levels)
    ]
    writes = [
        pltpu.make_async_copy(out.at[:, z], out_hbm.at[:, z], out_sems.at[z])
        for z in range(levels)
    ]
    for read in reads:
        read.start()
    reads[0].wait()
    row = iota((tile_x, tile_y), 0)
    lane = iota((tile_x, tile_y), 1)
    wind = 0.5 * time_step * advect_coef
    across = time_step * diffuse_h
    upward = time_step * diffuse_z
    keep = 1.0 - 4.0 * across - 2.0 * upward
    for z in range(levels):
        if z + 1 < levels:
            reads[z + 1].wait()
        u = wind * state[0, z]
        v = wind * state[1, z]
        east_gain = jnp.where(row == tile_x - 1, 0.0, across - u)
        west_gain = jnp.where(row == 0, 0.0, across + u)
        north_gain = jnp.where(lane == tile_y - 1, 0.0, across - v)
        south_gain = jnp.where(lane == 0, 0.0, across + v)
        for f in range(fields):
            cell = state[f, z]
            stacked = state[f, min(z + 1, levels - 1)] + state[f, max(z - 1, 0)]
            total = keep * cell + upward * stacked
            total = total + east_gain * pltpu.roll(cell, tile_x - 1, 0)
            total = total + west_gain * pltpu.roll(cell, 1, 0)
            total = total + north_gain * pltpu.roll(cell, tile_y - 1, 1)
            total = total + south_gain * pltpu.roll(cell, 1, 1)
            out[f, z] = total
        writes[z].start()
    for write in writes:
        write.wait()


def nudge_kernel(
    stages, flags_ref, bounds_ref, *refs
):
    sum_ref, recv_refs, refs = refs[0], refs[1 : 1 + stages], refs[1 + stages :]
    (terms_ref, gram_ref, ys_ref, wt_hi_ref, wt_lo_ref, own_first, own_last, south_ref, north_ref,
     base_hbm, out_hbm, num_ref, base, spread_ref, in_sem, out_sems) = refs
    kinds, tile_x, tile_y = base.shape
    levels = kinds // 3
    slots = ys_ref.shape[1]
    blocks = slots // RB
    read = pltpu.make_async_copy(base_hbm, base, in_sem)
    read.start()
    num_ref[...] = jnp.zeros_like(num_ref)
    total = sum_ref[0 : kinds + 1, :] + recv_refs[-1][0 : kinds + 1, :]
    averaged = total[0:kinds] / total[kinds : kinds + 1]
    spread_ref[0:kinds, :] = terms_ref[...] - dot(gram_ref[...], averaged, NN, HIGHEST)
    spread_ref[kinds : kinds + 1, :] = jnp.ones((1, slots), jnp.float32)

    for j in range(blocks):
        lanes = slice(j * RB, (j + 1) * RB)

        def add_pair(b, carry, lanes=lanes):
            start = pl.multiple_of(b * YB, YB)
            named = (iota((YB, RB), 0) + start).astype(jnp.float32) == ys_ref[0:1, lanes]
            spread = spread_ref[0 : kinds + 1, lanes]
            placed = jnp.where(named[None], spread[:, None, :], 0.0)
            b_hi, b_lo = split2(placed.reshape((kinds + 1) * YB, RB))
            w_hi, w_lo = wt_hi_ref[:, lanes], wt_lo_ref[:, lanes]
            part = dot(b_hi, w_hi, NT) + dot(b_hi, w_lo, NT) + dot(b_lo, w_hi, NT)
            num_ref[:, pl.ds(start, YB), :] += part.reshape(kinds + 1, YB, tile_x)
            return carry

        lax.fori_loop(bounds_ref[2 * j], bounds_ref[2 * j + 1], add_pair, 0)

    wind = 0.5 * time_step * advect_coef
    across = time_step * diffuse_h
    scale = time_step * nudge_gain / jnp.maximum(num_ref[kinds], 1.0)
    read.wait()
    for k in range(kinds):
        z = k % levels
        turned = num_ref[k] * scale
        south = south_ref[k : k + 1, :] * (across + wind * own_first[levels + z : levels + z + 1, :])
        north = north_ref[k : k + 1, :] * (across - wind * own_last[levels + z : levels + z + 1, :])
        cell_row = iota(turned.shape, 0)
        turned = turned + jnp.where(
            cell_row == 0, south, jnp.where(cell_row == tile_y - 1, north, 0.0)
        )
        base[k] = base[k] + jnp.transpose(turned)
        west = jnp.zeros((1, tile_y), jnp.float32)
        east = jnp.zeros((1, tile_y), jnp.float32)
        for s in range(stages):
            r, at = edge_place(slots, k, 1)
            west = west + jnp.where(flags_ref[2 * s] == 1, recv_refs[s][r : r + 1, at : at + LANES], 0.0)
            r, at = edge_place(slots, k, 0)
            east = east + jnp.where(flags_ref[2 * s + 1] == 1, recv_refs[s][r : r + 1, at : at + LANES], 0.0)
        r, at = edge_place(slots, z, 0)
        u_first = sum_ref[r : r + 1, at : at + LANES]
        r, at = edge_place(slots, z, 1)
        u_last = sum_ref[r : r + 1, at : at + LANES]
        base[k, 0:1, :] += west * (across + wind * u_first)
        base[k, tile_x - 1 : tile_x, :] += east * (across - wind * u_last)
        pltpu.make_async_copy(base.at[k], out_hbm.at[k], out_sems.at[k]).start()
    for k in range(kinds):
        pltpu.make_async_copy(base.at[k], out_hbm.at[k], out_sems.at[k]).wait()


def call(kernel, name, out_shape, in_specs, out_specs, scratch=(), flops=0, moved=0, **kwargs):
    return pl.pallas_call(
        kernel,
        name=name,
        out_shape=out_shape,
        in_specs=in_specs,
        out_specs=out_specs,
        scratch_shapes=list(scratch),
        compiler_params=pltpu.CompilerParams(vmem_limit_bytes=VMEM_LIMIT),
        cost_estimate=pl.CostEstimate(flops=flops, bytes_accessed=moved, transcendentals=0),
        **kwargs,
    )


def local(model_state, obs_val, obs_owner, obs_x, obs_y, cressman, vertical):
    count_x = lax.axis_size("gx")
    count_y = lax.axis_size("gy")
    fields, levels, tile_x, tile_y = model_state.shape
    kinds = fields * levels
    records = obs_val.shape[0]
    width = cressman.shape[0]
    cap = max(2, 2 * records // count_y)
    slots = count_x * count_y * cap
    blocks = slots // RB
    f32, bf16, i32 = jnp.float32, jnp.bfloat16, jnp.int32
    shape = jax.ShapeDtypeStruct
    stages = count_x.bit_length() - 1

    msg, gram = call(
        functools.partial(pack_kernel, count_y, cap),
        "pack_records",
        (shape((count_x * count_y, 8, LANES), f32), shape((kinds, kinds), f32)),
        [VMEM] * 5,
        (VMEM, VMEM),
        flops=10**7,
        moved=10**6,
    )(
        obs_owner.reshape(1, records),
        obs_x.reshape(1, records),
        obs_y.reshape(1, records),
        obs_val,
        vertical.reshape(kinds, vertical.shape[2]),
    )
    recv = lax.all_to_all(msg, ("gx", "gy"), split_axis=0, concat_axis=0, tiled=True)

    steps = 12
    planes, piece = kinds // steps, width // steps
    whole = lambda *dims: pl.BlockSpec(dims, lambda i: (0,) * len(dims))
    state3 = model_state.reshape(kinds, tile_x, tile_y)
    mt_hi, mt_lo, ct_hi, ct_lo, first_y, last_y, first_x, last_x = call(
        functools.partial(turn_kernel, planes),
        "turn_state",
        (
            shape((kinds, tile_y, tile_x), bf16),
            shape((kinds, tile_y, tile_x), bf16),
            shape((tile_x, width), bf16),
            shape((tile_x, width), bf16),
            shape((kinds, tile_x), f32),
            shape((kinds, tile_x), f32),
            shape((kinds, tile_y), f32),
            shape((kinds, tile_y), f32),
        ),
        [
            pl.BlockSpec((planes, tile_x, tile_y), lambda i: (i, 0, 0)),
            pl.BlockSpec((piece, tile_x), lambda i: (i, 0)),
        ],
        (
            pl.BlockSpec((planes, tile_y, tile_x), lambda i: (i, 0, 0)),
            pl.BlockSpec((planes, tile_y, tile_x), lambda i: (i, 0, 0)),
            pl.BlockSpec((tile_x, piece), lambda i: (0, i)),
            pl.BlockSpec((tile_x, piece), lambda i: (0, i)),
            whole(kinds, tile_x),
            whole(kinds, tile_x),
            whole(kinds, tile_y),
            whole(kinds, tile_y),
        ),
        grid=(steps,),
        moved=15 * 10**6,
    )(state3, cressman)

    up = [(i, i + 1) for i in range(count_y - 1)]
    down = [(i + 1, i) for i in range(count_y - 1)]
    south = lax.ppermute(last_y, "gy", up)
    north = lax.ppermute(first_y, "gy", down)

    partial, wt_hi, wt_lo, ys, terms, bounds = call(
        functools.partial(sums_kernel, cap, tile_y),
        "column_sums",
        (
            shape((WORDS, slots), f32),
            shape((tile_x, slots), bf16),
            shape((tile_x, slots), bf16),
            shape((8, slots), f32),
            shape((kinds, slots), f32),
            shape((2 * blocks,), i32),
        ),
        [VMEM] * 3 + [ANY] * 4,
        (VMEM, VMEM, VMEM, VMEM, VMEM, SMEM),
        [
            pltpu.VMEM((kinds, tile_y, tile_x), bf16),
            pltpu.VMEM((kinds, tile_y, tile_x), bf16),
            pltpu.VMEM((tile_x, width), bf16),
            pltpu.VMEM((tile_x, width), bf16),
            pltpu.VMEM((8, slots), f32),
            pltpu.VMEM((kinds, 8, RB), f32),
            pltpu.SemaphoreType.DMA((4,)),
        ],
        flops=4 * 10**9,
        moved=10**7,
    )(recv, first_x, last_x, mt_hi, mt_lo, ct_hi, ct_lo)

    summed, received = partial, []
    summing = (jnp.arange(WORDS) < kinds + 1)[:, None]
    for s in range(stages):
        mask = 2 ** (s + 1) - 1
        got = lax.ppermute(summed, "gx", [(i, i ^ mask) for i in range(count_x)])
        received.append(got)
        if s < stages - 1:
            summed = jnp.where(summing, summed + got, summed)

    base = call(
        stencil_kernel,
        "stencil",
        shape(model_state.shape, f32),
        [ANY],
        ANY,
        [
            pltpu.VMEM(model_state.shape, f32),
            pltpu.VMEM(model_state.shape, f32),
            pltpu.SemaphoreType.DMA((levels,)),
            pltpu.SemaphoreType.DMA((levels,)),
        ],
        moved=10**7,
    )(model_state)

    me = lax.axis_index("gx")
    flags = []
    for s in range(stages):
        partner = me ^ (2 ** (s + 1) - 1)
        flags += [partner == me - 1, partner == me + 1]
    flags = jnp.stack(flags).astype(i32)

    out = call(
        functools.partial(nudge_kernel, stages),
        "nudge",
        shape((kinds, tile_x, tile_y), f32),
        [SMEM, SMEM] + [VMEM] * (10 + stages) + [ANY],
        ANY,
        [
            pltpu.VMEM((kinds + 1, tile_y, tile_x), f32),
            pltpu.VMEM((kinds, tile_x, tile_y), f32),
            pltpu.VMEM((WORDS, slots), f32),
            pltpu.SemaphoreType.DMA,
            pltpu.SemaphoreType.DMA((kinds,)),
        ],
        flops=4 * 10**9,
        moved=10**7,
    )(
        flags, bounds, summed, *received, terms, gram, ys, wt_hi, wt_lo,
        first_y, last_y, south, north, base.reshape(kinds, tile_x, tile_y),
    )
    return out.reshape(model_state.shape)


def solution(mesh):
    in_specs = (
        P(None, None, "gx", "gy"),
        P(("gx", "gy"), None),
        P(("gx", "gy"), None),
        P(("gx", "gy")),
        P(("gx", "gy")),
        P(None, "gx"),
        P(),
    )
    out_specs = P(None, None, "gx", "gy")
    return jax.shard_map(local, mesh=mesh, in_specs=in_specs, out_specs=out_specs, check_vma=False)
```

profile of v0, /device:TPU:8, one launch (start us, length us, event | category | flops | bytes accessed | tf_op | source)
XLA Modules:
  0.0 60.6 jit_solution(7284515021809520071)
XLA Ops:
  0.0 0.0 copy-start.1
  0.0 0.9 %copy-done.1 = f32[128,384]{1,0:T(8,128)S(1)} copy-done((f32[128,384]{1,0:T(8,128)S(1)}, f32[128,384]{1,0:T(8,128)}, u32[]{:S(2)}) %copy-start.1) | copy-done | bytes 196632
  0.9 0.0 copy-start.2
  0.9 0.7 %copy-done.2 = f32[3,8,128]{2,1,0:T(8,128)S(1)} copy-done((f32[3,8,128]{2,1,0:T(8,128)S(1)}, f32[3,8,128]{2,1,0:T(8,128)}, u32[]{:S(2)}) %copy-start.2) | copy-done | bytes 12312
  1.6 0.0 copy-start.3
  1.6 0.7 %copy-done.3 = s32[128,1]{0,1:T(1,128)S(1)} copy-done((s32[128,1]{0,1:T(1,128)S(1)}, s32[128,1]{0,1:T(1,128)}, u32[]{:S(2)}) %copy-start.3) | copy-done | bytes 536
  2.3 0.0 copy-start.4
  2.3 0.7 %copy-done.4 = s32[128]{0:T(128)S(1)} copy-done((s32[128]{0:T(128)S(1)}, s32[128]{0:T(128)}, u32[]{:S(2)}) %copy-start.4) | copy-done | bytes 536
  2.9 0.7 %copy-done.5 = s32[128]{0:T(128)S(1)} copy-done((s32[128]{0:T(128)S(1)}, s32[128]{0:T(128)}, u32[]{:S(2)}) %copy-start.5) | copy-done | bytes 536
  3.6 1.5 %pack_records.1 = (f32[32,8,128]{2,1,0:T(8,128)}, f32[24,24]{1,0:T(8,128)S(1)}) custom-call(s32[1,128]{1,0:T(1,128)S(1)} %bitcast.13, s32[1,128]{1,0:T(1,128)S(1)} %bitcast.14, s32[1,128]{1,0:T(1,128)S(1)} %bitcast.15, f32[128,384]{1,0:T(8,128)S(1)} %copy-done.1, f32[24,128]{1,0:T(8,128)S(1)} %bitcast.12), custom_call_target="tpu_custom_call" | custom-call | flops 10000000 | bytes 1000000 | tf_op jit(solution)/shard_map/pack_records/pallas_call | solution.py:370
  5.1 6.0 %all-to-all-start = ((f32[32,8,128]{2,1,0:T(8,128)}), f32[32,8,128]{2,1,0:T(8,128)S(1)}, u32[]{:S(2)}, u32[]{:S(2)}) async-start(f32[32,8,128]{2,1,0:T(8,128)} %get-tuple-element.21), calls=%async_computation | async-start | bytes 262144 | tf_op jit(solution)/shard_map/all_to_all | solution.py:385
  11.2 9.3 %turn_state.1 = (bf16[24,128,384]{2,1,0:T(8,128)(2,1)S(1)}, bf16[24,128,384]{2,1,0:T(8,128)(2,1)}, bf16[384,1536]{1,0:T(8,128)(2,1)S(1)}, bf16[384,1536]{1,0:T(8...) custom-call(f32[24,384,128]{2,1,0:T(8,128)} %bitcast.16, ...), custom_call_target="tpu_custom_call" | custom-call | bytes 15000000 | tf_op jit(solution)/shard_map/turn_state/pallas_call | solution.py:391
  20.5 1.4 %copy-done.6 = bf16[24,128,384]{2,1,0:T(8,128)(2,1)} copy-done((bf16[24,128,384]{2,1,0:T(8,128)(2,1)}, bf16[24,128,384]{2,1,0:T(8,128)(2,1)S(1)}, u32[]{:S(2)}) %copy-start.6) | copy-done | bytes 2359320
  22.0 0.0 all-to-all-done.recv_ref
  22.0 11.6 %column_sums.1 = (f32[32,1024]{1,0:T(8,128)S(1)}, bf16[384,1024]{1,0:T(8,128)(2,1)S(1)}, bf16[384,1024]{1,0:T(8,128)(2,1)S(1)}, f32[8,1024]{1,0:T(8,128)S(1)}, f32[24,1024]{1,0:T(8,128)S(1)}, /*index=5*/s32[8]{0:T(128)S(1)}) custom-call(f32[32,8,128]{2,1,0:T(8,128)S(1)} %all-to-all-done.recv_ref, f32[24,128]{1,0:T(8,128)S(1)} %get-tuple-element.22.first_x_ref, ...), custom_call_target="tpu_custom_call" | custom-call | flops 4000000000 | bytes 10000000 | tf_op jit(solution)/shard_map/column_sums/pallas_call | solution.py:427
  33.6 0.0 copy-start.7
  33.6 0.9 %copy-done.7 = bf16[384,1024]{1,0:T(8,128)(2,1)} copy-done((bf16[384,1024]{1,0:T(8,128)(2,1)}, bf16[384,1024]{1,0:T(8,128)(2,1)S(1)}, u32[]{:S(2)}) %copy-start.7) | copy-done | bytes 786456
  34.5 0.2 collective-permute-start
  34.7 1.2 %collective-permute-done.refs_1_ = f32[32,1024]{1,0:T(8,128)S(1)} collective-permute-done((f32[32,1024]{1,0:T(8,128)S(1)}, f32[32,1024]{1,0:T(8,128)S(1)}, u32[]{:S(2)}, u32[]{:S(2)}) %collective-permute-start) | collective-permute-done | bytes 131104 | tf_op jit(solution)/shard_map/ppermute | solution.py:457
  35.8 0.1 add_select_fusion.refs_0_
  35.9 1.3 %collective-permute-start.1 = (f32[32,1024]{1,0:T(8,128)S(1)}, f32[32,1024]{1,0:T(8,128)S(1)}, u32[]{:S(2)}, u32[]{:S(2)}) collective-permute-start(f32[32,1024]{1,0:T(8,128)S(1)} %add_select_fusion.refs_0_), channel_id=1, source_target_pairs={{0,24},{8,16},{16,8},{24,0},{1,25},{9,17},{17,9},{25,1},{2,26},{10... | collective-permute-start | bytes 393224 | tf_op jit(solution)/shard_map/ppermute | solution.py:457
  37.2 3.4 %collective-permute-start.2 = (f32[24,384]{1,0:T(8,128)S(1)}, f32[24,384]{1,0:T(8,128)S(1)}, u32[]{:S(2)}, u32[]{:S(2)}) collective-permute-start(f32[24,384]{1,0:T(8,128)S(1)} %get-tuple-element.36.refs_9_), channel_id=1, source_target_pairs={{0,1},{1,2},{2,3},{3,4},{4,5},{5,6},{6,7},{8,9},{9,10},{10,11},{11... | collective-permute-start | bytes 110600 | tf_op jit(solution)/shard_map/ppermute | solution.py:424
  40.6 3.4 %collective-permute-start.3 = (f32[24,384]{1,0:T(8,128)S(1)}, f32[24,384]{1,0:T(8,128)S(1)}, u32[]{:S(2)}, u32[]{:S(2)}) collective-permute-start(f32[24,384]{1,0:T(8,128)S(1)} %get-tuple-element.35.refs_8_), channel_id=1, source_target_pairs={{1,0},{2,1},{3,2},{4,3},{5,4},{6,5},{7,6},{9,8},{10,9},{11,10},{12... | collective-permute-start | bytes 110600 | tf_op jit(solution)/shard_map/ppermute | solution.py:425
  44.0 0.1 add_convert_fusion.flags_ref
  44.1 5.1 %stencil.1 = f32[3,8,384,128]{3,2,1,0:T(8,128)S(1)} custom-call(f32[3,8,384,128]{3,2,1,0:T(8,128)} %state_hbm.1), custom_call_target="tpu_custom_call" | custom-call | bytes 10000000 | tf_op jit(solution)/shard_map/stencil/pallas_call | solution.py:462
  49.2 0.0 copy-start
  49.2 2.1 %copy-done = f32[3,8,384,128]{3,2,1,0:T(8,128)} copy-done((f32[3,8,384,128]{3,2,1,0:T(8,128)}, f32[3,8,384,128]{3,2,1,0:T(8,128)S(1)}, u32[]{:S(2)}) %copy-start) | copy-done | bytes 4718616
  51.4 0.0 collective-permute-done.2.refs_10_
  51.4 0.0 collective-permute-done.3.refs_11_
  51.4 0.0 collective-permute-done.1.refs_2_
  51.4 0.0 copy-done.8
  51.4 9.2 %nudge.1 = f32[24,384,128]{2,1,0:T(8,128)} custom-call(s32[4]{0:T(128)S(1)} %add_convert_fusion.flags_ref, s32[8]{0:T(128)S(1)} %get-tuple-element.28.bounds_ref, f32[32,1024]{1,0:T(8,128)S(1)} %add_select_fusion.refs_0_, f32[32,1024]{1,0:T(8,128)S(1)} %collective-permute-done.refs_1_, f32[32,1024]{1,0:T(8,128)S(1)} %collective-permute-done.1.refs_2_, ...), custom_call_target="tpu_custom_call" | custom-call | flops 4000000000 | bytes 10000000 | tf_op jit(solution)/shard_map/nudge/pallas_call | solution.py:484
  (4 shorter events, 0.0 us)
Async XLA Ops:
  0.0 0.9 %copy-start.1 = (f32[128,384]{1,0:T(8,128)S(1)}, f32[128,384]{1,0:T(8,128)}, u32[]{:S(2)}) copy-start(f32[128,384]{1,0:T(8,128)} %obs_ref.1) | copy-start | bytes 589828
  0.9 0.7 %copy-start.2 = (f32[3,8,128]{2,1,0:T(8,128)S(1)}, f32[3,8,128]{2,1,0:T(8,128)}, u32[]{:S(2)}) copy-start(f32[3,8,128]{2,1,0:T(8,128)} %param.13) | copy-start | bytes 36868
  1.6 0.7 %copy-start.3 = (s32[128,1]{0,1:T(1,128)S(1)}, s32[128,1]{0,1:T(1,128)}, u32[]{:S(2)}) copy-start(s32[128,1]{0,1:T(1,128)} %param.9) | copy-start | bytes 1540
  2.3 0.7 %copy-start.4 = (s32[128]{0:T(128)S(1)}, s32[128]{0:T(128)}, u32[]{:S(2)}) copy-start(s32[128]{0:T(128)} %param.10) | copy-start | bytes 1540
  2.9 0.7 %copy-start.5 = (s32[128]{0:T(128)S(1)}, s32[128]{0:T(128)}, u32[]{:S(2)}) copy-start(s32[128]{0:T(128)} %param.11) | copy-start | bytes 1540
  5.1 16.8 %all-to-all-start = ((f32[32,8,128]{2,1,0:T(8,128)}), f32[32,8,128]{2,1,0:T(8,128)S(1)}, u32[]{:S(2)}, u32[]{:S(2)}) async-start(f32[32,8,128]{2,1,0:T(8,128)} %get-tuple-element.21), calls=%async_computation | async-start | bytes 262144 | tf_op jit(solution)/shard_map/all_to_all | solution.py:385
  20.5 1.4 %copy-start.6 = (bf16[24,128,384]{2,1,0:T(8,128)(2,1)}, bf16[24,128,384]{2,1,0:T(8,128)(2,1)S(1)}, u32[]{:S(2)}) copy-start(bf16[24,128,384]{2,1,0:T(8,128)(2,1)S(1)} %get-tuple-element.24.mt_hi_hbm) | copy-start | bytes 7077892
  33.6 0.9 %copy-start.7 = (bf16[384,1024]{1,0:T(8,128)(2,1)}, bf16[384,1024]{1,0:T(8,128)(2,1)S(1)}, u32[]{:S(2)}) copy-start(bf16[384,1024]{1,0:T(8,128)(2,1)S(1)} %get-tuple-element.34.refs_7_) | copy-start | bytes 2359300
  34.5 1.3 %collective-permute-start = (f32[32,1024]{1,0:T(8,128)S(1)}, f32[32,1024]{1,0:T(8,128)S(1)}, u32[]{:S(2)}, u32[]{:S(2)}) collective-permute-start(f32[32,1024]{1,0:T(8,128)S(1)} %get-tuple-element.29), channel_id=1, source_target_pairs={{0,8},{8,0},{16,24},{24,16},{1,9},{9,1},{17,25},{25,17},{2,10},{10... | collective-permute-start | bytes 393224 | tf_op jit(solution)/shard_map/ppermute | solution.py:457
  35.9 15.4 %collective-permute-start.1 = (f32[32,1024]{1,0:T(8,128)S(1)}, f32[32,1024]{1,0:T(8,128)S(1)}, u32[]{:S(2)}, u32[]{:S(2)}) collective-permute-start(f32[32,1024]{1,0:T(8,128)S(1)} %add_select_fusion.refs_0_), channel_id=1, source_target_pairs={{0,24},{8,16},{16,8},{24,0},{1,25},{9,17},{17,9},{25,1},{2,26},{10... | collective-permute-start | bytes 393224 | tf_op jit(solution)/shard_map/ppermute | solution.py:457
  37.2 14.1 %collective-permute-start.2 = (f32[24,384]{1,0:T(8,128)S(1)}, f32[24,384]{1,0:T(8,128)S(1)}, u32[]{:S(2)}, u32[]{:S(2)}) collective-permute-start(f32[24,384]{1,0:T(8,128)S(1)} %get-tuple-element.36.refs_9_), channel_id=1, source_target_pairs={{0,1},{1,2},{2,3},{3,4},{4,5},{5,6},{6,7},{8,9},{9,10},{10,11},{11... | collective-permute-start | bytes 110600 | tf_op jit(solution)/shard_map/ppermute | solution.py:424
  40.6 10.8 %collective-permute-start.3 = (f32[24,384]{1,0:T(8,128)S(1)}, f32[24,384]{1,0:T(8,128)S(1)}, u32[]{:S(2)}, u32[]{:S(2)}) collective-permute-start(f32[24,384]{1,0:T(8,128)S(1)} %get-tuple-element.35.refs_8_), channel_id=1, source_target_pairs={{1,0},{2,1},{3,2},{4,3},{5,4},{6,5},{7,6},{9,8},{10,9},{11,10},{12... | collective-permute-start | bytes 110600 | tf_op jit(solution)/shard_map/ppermute | solution.py:425
  44.1 7.3 %copy-start.8 = (bf16[384,1024]{1,0:T(8,128)(2,1)S(1)}, bf16[384,1024]{1,0:T(8,128)(2,1)}, u32[]{:S(2)}) copy-start(bf16[384,1024]{1,0:T(8,128)(2,1)} %copy-done.7) | copy-start | bytes 2359300
  49.2 2.1 %copy-start = (f32[3,8,384,128]{3,2,1,0:T(8,128)}, f32[3,8,384,128]{3,2,1,0:T(8,128)S(1)}, u32[]{:S(2)}) copy-start(f32[3,8,384,128]{3,2,1,0:T(8,128)S(1)} %stencil.1) | copy-start | bytes 14155780
where the time goes:
time: 60.7 us; the launch traced here: 60.6 us
  Pallas kernels  36.9 us (61%)
  starting transfers between devices  14.2 us (23%)
  local copies, waits for them, and re-layouts  8.03 us (13%)
  waiting for transfers between devices  1.2 us (2%)
    pallas_call x1, Pallas kernels, local(): call(functools.partial(sums_kernel, cap, tile_y), 'column_sums', (shape((...  11.6 us
    pallas_call x1, Pallas kernels, local(): call(functools.partial(turn_kernel, planes), 'turn_state', (shape((kinds,...  9.34 us
    pallas_call x1, Pallas kernels, local(): call(functools.partial(nudge_kernel, stages), 'nudge', shape((kinds, tile...  9.25 us
    unnamed x18, local copies, waits for them, and re-layouts  8.03 us
    all_to_all x1, starting transfers between devices, local(): lax.all_to_all(msg, ('gx', 'gy'), split_axis=0, concat_axis=0, tiled=True)  6.04 us
    pallas_call x1, Pallas kernels, local(): call(stencil_kernel, 'stencil', shape(model_state.shape, f32), [ANY], ANY...  5.15 us
    ppermute x1, starting transfers between devices, local(): north = lax.ppermute(first_y, 'gy', down)  3.37 us
    ppermute x1, starting transfers between devices, local(): south = lax.ppermute(last_y, 'gy', up)  3.37 us
  transfers between devices with their start and end apart: 5, of which 1 were waited for; matrix products, arithmetic and copies ran while one was open for 0% of the time, Pallas kernels for 24%

commit v1 on v0

v1 whole, which is shorter than its diff:
```python
import functools

import jax
import jax.numpy as jnp
from jax import lax
from jax.experimental import pallas as pl
from jax.experimental.pallas import tpu as pltpu
from jax.sharding import PartitionSpec as P

advect_coef = 0.5
diffuse_h = 0.2
diffuse_z = 0.1
time_step = 0.5
nudge_gain = 1.0
spread_gain = 0.125

LANES = 128
WORDS = 32
LANE_STEP = 32
YB = 16
RB = 256
MIB = 1024 * 1024
MOST = 58
SOME = 50

HIGHEST = lax.Precision.HIGHEST
NT = (((1,), (1,)), ((), ()))
NN = (((1,), (0,)), ((), ()))
VMEM = pl.BlockSpec(memory_space=pltpu.VMEM)
ANY = pl.BlockSpec(memory_space=pl.ANY)
SMEM = pl.BlockSpec(memory_space=pltpu.SMEM)
HBM = pl.BlockSpec(memory_space=pltpu.HBM)


def dot(a, b, dims=NN, precision=None):
    return lax.dot_general(a, b, dims, precision=precision, preferred_element_type=jnp.float32)


def split2(value):
    high = value.astype(jnp.bfloat16)
    low = (value - high.astype(jnp.float32)).astype(jnp.bfloat16)
    return high, low


def iota(shape, axis):
    return lax.broadcasted_iota(jnp.int32, shape, axis)


def pack_kernel(count_y, cap, *refs):
    sources, (msg_ref, gram_ref), places, sems = refs[:5], refs[5:7], refs[7:12], refs[12]
    copies = [pltpu.make_async_copy(a, b, sems.at[i]) for i, (a, b) in enumerate(zip(sources, places))]
    for copy in copies:
        copy.start()
    for copy in copies:
        copy.wait()
    owner_ref, x_ref, y_ref, obs_ref, vert_ref = places
    records, kinds = x_ref.shape[1], vert_ref.shape[0]
    levels = kinds // 3
    vert = vert_ref[...]
    terms = []
    for v in range(3):
        obs = obs_ref[:, v * LANES : (v + 1) * LANES]
        terms.append(dot(vert[v * levels : (v + 1) * levels], obs, NT, HIGHEST) * spread_gain)
    row = iota((8, records), 0)
    x_row = jnp.broadcast_to(x_ref[...].astype(jnp.float32), (8, records))
    y_row = jnp.broadcast_to(y_ref[...].astype(jnp.float32) - float(LANES), (8, records))
    head = jnp.where(row == 0, x_row, jnp.where(row == 1, y_row, 0.0))
    payload = jnp.concatenate([head] + terms, axis=0)

    owner = owner_ref[...].astype(jnp.float32)
    owner_lanes = jnp.broadcast_to(owner, (records, records))
    owner_rows = jnp.transpose(owner_lanes)
    earlier = iota((records, records), 0) < iota((records, records), 1)
    same = jnp.where((owner_lanes == owner_rows) & earlier, 1.0, 0.0)
    rank = jnp.sum(same, axis=0, keepdims=True)
    slot = owner * float(cap) + rank
    places = count_y * cap
    pick = jnp.where(iota((places, records), 0).astype(jnp.float32) == slot, 1.0, 0.0)
    out = dot(payload, pick, NT, HIGHEST)

    lane = iota((8, LANES), 1)
    for c in range(count_y):
        chunk = (c * cap) // LANES
        offset = (c * cap) % LANES
        block = jnp.zeros((8, LANES), jnp.float32)
        for j in range(WORDS // 8):
            part = out[8 * j : 8 * j + 8, chunk * LANES : (chunk + 1) * LANES]
            shift = (LANE_STEP * j - offset) % LANES
            if shift:
                part = pltpu.roll(part, shift, 1)
            inside = (lane >= LANE_STEP * j) & (lane < LANE_STEP * j + cap)
            block = jnp.where(inside, part, block)
        for g in range(msg_ref.shape[0] // count_y):
            msg_ref[g * count_y + c] = block

    gram = dot(vert, vert, NT, HIGHEST) * spread_gain
    alike = (iota((kinds, kinds), 0) // levels) == (iota((kinds, kinds), 1) // levels)
    gram_ref[...] = jnp.where(alike, gram, 0.0)


def unpack(recv_ref, cap, j):
    devices = recv_ref.shape[0]
    per = LANES // cap
    lane = iota((8, LANES), 1)
    chunks = []
    for q in range(devices // per):
        block = jnp.zeros((8, LANES), jnp.float32)
        for t in range(per):
            part = recv_ref[q * per + t]
            shift = (cap * t - LANE_STEP * j) % LANES
            if shift:
                part = pltpu.roll(part, shift, 1)
            inside = (lane >= cap * t) & (lane < cap * t + cap)
            block = jnp.where(inside, part, block)
        chunks.append(block)
    return chunks


def pair_list(bounds_ref, blocks, y_blocks):
    j, b = jnp.int32(0), bounds_ref[0]
    pairs = []
    for _ in range(blocks + y_blocks - 1):
        valid = (j < blocks) & (b < bounds_ref[2 * jnp.minimum(j, blocks - 1) + 1])
        pairs.append((jnp.minimum(j, blocks - 1), jnp.where(valid, b, y_blocks + 1)))
        more = b + 1 < bounds_ref[2 * jnp.minimum(j, blocks - 1) + 1]
        following = jnp.minimum(j + 1, blocks - 1)
        b = jnp.where(more, b + 1, bounds_ref[2 * following])
        j = jnp.where(more, j, jnp.minimum(j + 1, blocks))
    return pairs


def edge_place(slots, k, side):
    per = slots // LANES
    rows = -(-24 // per)
    return 25 + side * rows + k // per, (k % per) * LANES


def sums_kernel(
    cap, recv_ref, edge_hbm, state_hbm, cress_hbm,
    msg_ref, wt_ref, ys_ref, terms_ref, bounds_ref, give_a_ref, give_b_ref,
    acc_ref, edge_ref, state, cress, mt_hi, mt_lo, ct, sems, edge_sem,
):
    kinds, tile_x, tile_y = state.shape
    width = cress.shape[0]
    blocks = recv_ref.shape[0] * cap // RB
    piece, planes = width // blocks, kinds // blocks
    cress_reads, state_reads = [], []
    for i in range(blocks):
        rows, some = pl.ds(i * piece, piece), pl.ds(i * planes, planes)
        cress_reads.append(pltpu.make_async_copy(cress_hbm.at[rows], cress.at[rows], sems.at[i]))
        state_reads.append(pltpu.make_async_copy(state_hbm.at[some], state.at[some], sems.at[blocks + i]))
    for read in cress_reads:
        read.start()
    slots = recv_ref.shape[0] * cap
    chunks = slots // LANES

    groups = [unpack(recv_ref, cap, j) for j in range(WORDS // 8)]
    keys = []
    for c in range(chunks):
        place = (iota((1, LANES), 1) + c * LANES).astype(jnp.float32)
        keys.append((groups[0][c][1:2] + float(tile_y)) * float(slots) + place)
    counts = [jnp.zeros((8, LANES), jnp.float32) for _ in range(chunks)]
    for c in range(chunks):
        column = jnp.transpose(jnp.broadcast_to(keys[c], (LANES, LANES)))
        for d in range(chunks):
            less = jnp.where(column < keys[d], 1.0, 0.0)
            counts[d] = counts[d] + jnp.sum(less.reshape(LANES // 8, 8, LANES), axis=0)
    rank = jnp.concatenate([jnp.sum(count, axis=0, keepdims=True) for count in counts], axis=1)

    rows = []
    head = jnp.concatenate(groups[0], axis=1)
    x_high = jnp.floor(head[0:1] * 0.0625)
    row = iota((8, slots), 0)
    top = jnp.where(
        row == 0,
        jnp.broadcast_to(x_high, (8, slots)),
        jnp.where(
            row == 1,
            jnp.broadcast_to(head[0:1] - 16.0 * x_high, (8, slots)),
            jnp.where(row == 2, jnp.broadcast_to(head[1:2] + float(tile_y), (8, slots)), 0.0),
        ),
    )
    words = jnp.concatenate([jnp.concatenate(group, axis=1) for group in groups[1:]], axis=0)
    high = words.astype(jnp.bfloat16).astype(jnp.float32)
    middle = (words - high).astype(jnp.bfloat16).astype(jnp.float32)
    low = words - high - middle
    table = jnp.concatenate([top, high, middle, low], axis=0).astype(jnp.bfloat16)

    for read in state_reads:
        read.start()
    even = lax.rem(lax.axis_index("gy"), 2) == 0
    edge_read = pltpu.make_async_copy(edge_hbm, edge_ref, edge_sem)
    edge_read.start()
    x_rows = []
    for j in range(blocks):
        lanes = slice(j * RB, (j + 1) * RB)
        place = (iota((RB, slots), 0) + j * RB).astype(jnp.float32)
        pick = jnp.where(place == rank, 1.0, 0.0).astype(jnp.bfloat16)
        ordered = dot(table, pick, NT)
        x_rows.append(ordered[0:1] * 16.0 + ordered[1:2])
        ys = ordered[2:3]
        ys_ref[:, lanes] = jnp.broadcast_to(ys, (8, RB))
        terms_ref[:, lanes] = ordered[8:32] + ordered[32:56] + ordered[56:80]
        least = jnp.min(ys).astype(jnp.int32)
        most = jnp.minimum(jnp.max(ys).astype(jnp.int32), tile_y - 1)
        bounds_ref[2 * j] = least // YB
        bounds_ref[2 * j + 1] = most // YB + 1

    for read in cress_reads:
        read.wait()
    for i in range(width // LANES):
        rows = slice(i * LANES, (i + 1) * LANES)
        high, low = split2(jnp.transpose(cress[rows, :]))
        ct[0:tile_x, rows] = high
        ct[tile_x:, rows] = low

    def gather(j):
        hot = jnp.where(iota((width, RB), 0).astype(jnp.float32) == x_rows[j], 1.0, 0.0)
        wt = dot(ct[...], hot.astype(jnp.bfloat16))
        wt_ref[:, j * RB : (j + 1) * RB] = wt.astype(jnp.bfloat16)

    half = blocks // 2
    for j in range(half):
        gather(j)
    for read in state_reads:
        read.wait()
    planes = kinds // (blocks - half)
    for j in range(half, blocks):
        gather(j)
        for k in range((j - half) * planes, (j - half + 1) * planes):
            turned = jnp.transpose(state[k])
            high, low = split2(turned)
            mt_hi[k] = high
            mt_lo[k] = low
            first, last = turned[0:1], turned[tile_y - 1 :]
            give_a_ref[k : k + 1, :] = jnp.where(even, last, first)
            give_b_ref[k : k + 1, :] = jnp.where(even, first, last)

    acc_ref[...] = jnp.zeros_like(acc_ref)
    y_blocks = tile_y // YB
    for j, b in pair_list(bounds_ref, blocks, y_blocks):
        lanes = pl.ds(pl.multiple_of(j * RB, RB), RB)
        start = pl.multiple_of(jnp.minimum(b, y_blocks - 1) * YB, YB)
        a_hi = mt_hi[:, pl.ds(start, YB), :].reshape(kinds * YB, tile_x)
        a_lo = mt_lo[:, pl.ds(start, YB), :].reshape(kinds * YB, tile_x)
        w_hi = wt_ref[0:tile_x, lanes]
        part = dot(jnp.concatenate([a_hi, a_hi], axis=1), wt_ref[:, lanes]) + dot(a_lo, w_hi)
        named = (iota((YB, RB), 0) + b * YB).astype(jnp.float32) == ys_ref[0:1, lanes]
        kept = jnp.where(named[None], part.reshape(kinds, YB, RB), 0.0)
        acc_ref[j] += kept[:, :8] + kept[:, 8:]

    ones = jnp.ones((8, 2 * tile_x), jnp.bfloat16)
    for j in range(blocks):
        lanes = slice(j * RB, (j + 1) * RB)
        msg_ref[0:kinds, lanes] = jnp.sum(acc_ref[j], axis=1)
        total = dot(ones, wt_ref[:, lanes])
        msg_ref[kinds : kinds + 1, lanes] = total[0:1]
    msg_ref[kinds + 1 :, :] = jnp.zeros((WORDS - kinds - 1, slots), jnp.float32)
    edge_read.wait()
    for side in range(2):
        for k in range(kinds):
            r, at = edge_place(slots, k, side)
            msg_ref[r : r + 1, at : at + LANES] = edge_ref[side, k : k + 1, :]


def stencil_kernel(state_hbm, out_hbm, edge_ref, state, out, sems, out_sems):
    fields, levels, tile_x, tile_y = state.shape
    reads = [
        pltpu.make_async_copy(state_hbm.at[:, z], state.at[:, z], sems.at[z]) for z in range(levels)
    ]
    writes = [
        pltpu.make_async_copy(out.at[:, z], out_hbm.at[:, z], out_sems.at[z]) for z in range(levels)
    ]
    for read in reads:
        read.start()
    reads[0].wait()
    row = iota((tile_x, tile_y), 0)
    lane = iota((tile_x, tile_y), 1)
    wind = 0.5 * time_step * advect_coef
    across = time_step * diffuse_h
    upward = time_step * diffuse_z
    keep = 1.0 - 4.0 * across - 2.0 * upward
    for z in range(levels):
        if z + 1 < levels:
            reads[z + 1].wait()
        u = wind * state[0, z]
        v = wind * state[1, z]
        east_gain = jnp.where(row == tile_x - 1, 0.0, across - u)
        west_gain = jnp.where(row == 0, 0.0, across + u)
        north_gain = jnp.where(lane == tile_y - 1, 0.0, across - v)
        south_gain = jnp.where(lane == 0, 0.0, across + v)
        for f in range(fields):
            cell = state[f, z]
            edge_ref[0, f * levels + z : f * levels + z + 1, :] = cell[0:1]
            edge_ref[1, f * levels + z : f * levels + z + 1, :] = cell[tile_x - 1 :]
            stacked = state[f, min(z + 1, levels - 1)] + state[f, max(z - 1, 0)]
            total = keep * cell + upward * stacked
            total = total + east_gain * pltpu.roll(cell, tile_x - 1, 0)
            total = total + west_gain * pltpu.roll(cell, 1, 0)
            total = total + north_gain * pltpu.roll(cell, tile_y - 1, 1)
            total = total + south_gain * pltpu.roll(cell, 1, 1)
            out[f, z] = total
        writes[z].start()
    for write in writes:
        write.wait()


def nudge_kernel(stages, bounds_ref, *refs):
    me = lax.axis_index("gx")
    even = lax.rem(lax.axis_index("gy"), 2) == 0
    sum_ref, recv_refs, refs = refs[0], refs[1 : 1 + stages], refs[1 + stages :]
    (terms_ref, gram_ref, ys_ref, wt_ref, give_a, give_b, got_a, got_b,
     base_hbm, out_hbm, num_ref, base, out, spread_ref, in_sem, out_sems) = refs
    kinds, tile_x, tile_y = base.shape
    levels = kinds // 3
    slots = ys_ref.shape[1]
    blocks = slots // RB
    read = pltpu.make_async_copy(base_hbm, base, in_sem)
    read.start()
    num_ref[...] = jnp.zeros_like(num_ref)
    total = sum_ref[0 : kinds + 1, :] + recv_refs[-1][0 : kinds + 1, :]
    averaged = total[0:kinds] / total[kinds : kinds + 1]
    spread_ref[0:kinds, :] = terms_ref[...] - dot(gram_ref[...], averaged, NN, HIGHEST)
    spread_ref[kinds : kinds + 1, :] = jnp.ones((1, slots), jnp.float32)

    y_blocks = tile_y // YB
    for j, b in pair_list(bounds_ref, blocks, y_blocks):
        lanes = pl.ds(pl.multiple_of(j * RB, RB), RB)
        start = pl.multiple_of(jnp.minimum(b, y_blocks - 1) * YB, YB)
        named = (iota((YB, RB), 0) + b * YB).astype(jnp.float32) == ys_ref[0:1, lanes]
        spread = spread_ref[0 : kinds + 1, lanes]
        placed = jnp.where(named[None], spread[:, None, :], 0.0)
        b_hi, b_lo = split2(placed.reshape((kinds + 1) * YB, RB))
        both = dot(b_hi, wt_ref[:, lanes], NT)
        part = both[:, 0:tile_x] + both[:, tile_x:] + dot(b_lo, wt_ref[0:tile_x, lanes], NT)
        num_ref[:, pl.ds(start, YB), :] += part.reshape(kinds + 1, YB, tile_x)

    wind = 0.5 * time_step * advect_coef
    across = time_step * diffuse_h
    scale = time_step * nudge_gain / jnp.maximum(num_ref[kinds], 1.0)
    read.wait()
    for k in range(kinds):
        z = k % levels
        turned = num_ref[k] * scale
        v_row = slice(levels + z, levels + z + 1)
        beyond_a, beyond_b = got_a[k : k + 1, :], got_b[k : k + 1, :]
        v_a, v_b = give_a[v_row, :], give_b[v_row, :]
        north = jnp.where(even, beyond_a, beyond_b) * (across - wind * jnp.where(even, v_a, v_b))
        south = jnp.where(even, beyond_b, beyond_a) * (across + wind * jnp.where(even, v_b, v_a))
        cell_row = iota(turned.shape, 0)
        turned = turned + jnp.where(
            cell_row == 0, south, jnp.where(cell_row == tile_y - 1, north, 0.0)
        )
        out[k] = base[k] + jnp.transpose(turned)
        west = jnp.zeros((1, tile_y), jnp.float32)
        east = jnp.zeros((1, tile_y), jnp.float32)
        for s in range(stages):
            r, at = edge_place(slots, k, 1)
            west = west + jnp.where(me ^ (2 ** (s + 1) - 1) == me - 1, recv_refs[s][r : r + 1, at : at + LANES], 0.0)
            r, at = edge_place(slots, k, 0)
            east = east + jnp.where(me ^ (2 ** (s + 1) - 1) == me + 1, recv_refs[s][r : r + 1, at : at + LANES], 0.0)
        r, at = edge_place(slots, z, 0)
        u_first = sum_ref[r : r + 1, at : at + LANES]
        r, at = edge_place(slots, z, 1)
        u_last = sum_ref[r : r + 1, at : at + LANES]
        out[k, 0:1, :] += west * (across + wind * u_first)
        out[k, tile_x - 1 : tile_x, :] += east * (across - wind * u_last)
        pltpu.make_async_copy(out.at[k], out_hbm.at[k], out_sems.at[k]).start()
    for k in range(kinds):
        pltpu.make_async_copy(out.at[k], out_hbm.at[k], out_sems.at[k]).wait()


def call(kernel, name, out_shape, in_specs, out_specs, scratch=(), vmem=8, flops=0, moved=0):
    return pl.pallas_call(
        kernel,
        name=name,
        out_shape=out_shape,
        in_specs=in_specs,
        out_specs=out_specs,
        scratch_shapes=list(scratch),
        compiler_params=pltpu.CompilerParams(vmem_limit_bytes=vmem * MIB),
        cost_estimate=pl.CostEstimate(flops=flops, bytes_accessed=moved, transcendentals=0),
    )


def local(model_state, obs_val, obs_owner, obs_x, obs_y, cressman, vertical):
    count_x = lax.axis_size("gx")
    count_y = lax.axis_size("gy")
    fields, levels, tile_x, tile_y = model_state.shape
    kinds = fields * levels
    records = obs_val.shape[0]
    width = cressman.shape[0]
    cap = max(2, 2 * records // count_y)
    slots = count_x * count_y * cap
    blocks = slots // RB
    f32, bf16, i32 = jnp.float32, jnp.bfloat16, jnp.int32
    shape = jax.ShapeDtypeStruct
    stages = count_x.bit_length() - 1

    msg, gram = call(
        functools.partial(pack_kernel, count_y, cap),
        "pack_records",
        (shape((count_x * count_y, 8, LANES), f32), shape((kinds, kinds), f32)),
        [HBM] * 5,
        (VMEM, VMEM),
        [pltpu.VMEM((1, records), i32)] * 3
        + [
            pltpu.VMEM(obs_val.shape, f32),
            pltpu.VMEM((kinds, vertical.shape[2]), f32),
            pltpu.SemaphoreType.DMA((5,)),
        ],
        vmem=MOST,
        flops=10**7,
        moved=10**6,
    )(
        obs_owner.reshape(1, records),
        obs_x.reshape(1, records),
        obs_y.reshape(1, records),
        obs_val,
        vertical.reshape(kinds, vertical.shape[2]),
    )
    recv = lax.all_to_all(msg, ("gx", "gy"), split_axis=0, concat_axis=0, tiled=True)

    base, edges = call(
        stencil_kernel,
        "stencil",
        (shape(model_state.shape, f32), shape((2, kinds, tile_y), f32)),
        [HBM],
        (HBM, VMEM),
        [
            pltpu.VMEM(model_state.shape, f32),
            pltpu.VMEM(model_state.shape, f32),
            pltpu.SemaphoreType.DMA((levels,)),
            pltpu.SemaphoreType.DMA((levels,)),
        ],
        vmem=MOST,
        moved=10**7,
    )(model_state)

    state3 = model_state.reshape(kinds, tile_x, tile_y)
    partial, wt, ys, terms, bounds, give_a, give_b = call(
        functools.partial(sums_kernel, cap),
        "column_sums",
        (
            shape((WORDS, slots), f32),
            shape((2 * tile_x, slots), bf16),
            shape((8, slots), f32),
            shape((kinds, slots), f32),
            shape((2 * blocks,), i32),
            shape((kinds, tile_x), f32),
            shape((kinds, tile_x), f32),
        ),
        [VMEM, HBM, HBM, HBM],
        (VMEM, VMEM, VMEM, VMEM, SMEM, VMEM, VMEM),
        [
            pltpu.VMEM((blocks, kinds, 8, RB), f32),
            pltpu.VMEM((2, kinds, tile_y), f32),
            pltpu.VMEM((kinds, tile_x, tile_y), f32),
            pltpu.VMEM((width, tile_x), f32),
            pltpu.VMEM((kinds, tile_y, tile_x), bf16),
            pltpu.VMEM((kinds, tile_y, tile_x), bf16),
            pltpu.VMEM((2 * tile_x, width), bf16),
            pltpu.SemaphoreType.DMA((2 * blocks,)),
            pltpu.SemaphoreType.DMA,
        ],
        vmem=SOME,
        flops=4 * 10**9,
        moved=10**7,
    )(recv, edges, state3, cressman)

    got_a = lax.ppermute(give_a, "gy", [(i, i ^ 1) for i in range(count_y)])
    got_b = lax.ppermute(give_b, "gy", [(i, ((i - 1) ^ 1) + 1) for i in range(1, count_y - 1)])

    summed, received = partial, []
    summing = (jnp.arange(WORDS) < kinds + 1)[:, None]
    for s in range(stages):
        mask = 2 ** (s + 1) - 1
        got = lax.ppermute(summed, "gx", [(i, i ^ mask) for i in range(count_x)])
        received.append(got)
        if s < stages - 1:
            summed = jnp.where(summing, summed + got, summed)

    out = call(
        functools.partial(nudge_kernel, stages),
        "nudge",
        shape((kinds, tile_x, tile_y), f32),
        [SMEM] + [VMEM] * (9 + stages) + [HBM],
        ANY,
        [
            pltpu.VMEM((kinds + 1, tile_y, tile_x), f32),
            pltpu.VMEM((kinds, tile_x, tile_y), f32),
            pltpu.VMEM((kinds, tile_x, tile_y), f32),
            pltpu.VMEM((WORDS, slots), f32),
            pltpu.SemaphoreType.DMA,
            pltpu.SemaphoreType.DMA((kinds,)),
        ],
        vmem=SOME,
        flops=4 * 10**9,
        moved=10**7,
    )(
        bounds, summed, *received, terms, gram, ys, wt,
        give_a, give_b, got_a, got_b, base.reshape(kinds, tile_x, tile_y),
    )
    return out.reshape(model_state.shape)


def solution(mesh):
    in_specs = (
        P(None, None, "gx", "gy"),
        P(("gx", "gy"), None),
        P(("gx", "gy"), None),
        P(("gx", "gy")),
        P(("gx", "gy")),
        P(None, "gx"),
        P(),
    )
    out_specs = P(None, None, "gx", "gy")
    return jax.shard_map(local, mesh=mesh, in_specs=in_specs, out_specs=out_specs, check_vma=False)
```

time: 60.7 us -> 44.5 us (0.73)
  Pallas kernels: 36.9 us -> 26.1 us
  local copies, waits for them, and re-layouts: 8.03 us -> 0.74 us
  waiting for transfers between devices: 1.2 us -> 5.44 us
  starting transfers between devices: 14.2 us -> 11.6 us
    pallas_call x3 -> x2, Pallas kernels: 26.1 us -> 15 us  [the longest x1 8.85 us: local(): call(functools.partial(sums_kernel, cap), 'column_sums', (shape((WORDS, s...]
    unnamed x18 -> x4, local copies, waits for them, and re-layouts: 8.03 us -> 0.74 us
    ppermute x2, waiting for transfers between devices: 0.01 us -> 3.31 us  [the longest x1 3.31 us: local(): lax.ppermute(give_b, 'gy', [(i, (i - 1 ^ 1) + 1) for i in range(1, count_...]
    ppermute x2, starting transfers between devices: 6.74 us -> 4.95 us  [the longest x1 3.41 us: local(): lax.ppermute(give_b, 'gy', [(i, (i - 1 ^ 1) + 1) for i in range(1, count_...]
    pallas_call x1, Pallas kernels: 1.54 us -> 2.57 us  [local(): call(functools.partial(pack_kernel, count_y, cap), 'pack_records', (shape...]
    ppermute x2, starting transfers between devices: 1.44 us -> 0.6 us  [local(): got = lax.ppermute(summed, 'gx', [(i, i ^ mask) for i in range(count_x)])]
    all_to_all x1, waiting for transfers between devices: 0.01 us -> 0.81 us  [local(): lax.all_to_all(msg, ('gx', 'gy'), split_axis=0, concat_axis=0, tiled=True)]
    pallas_call x1, Pallas kernels: 9.25 us -> 8.47 us  [local(): call(functools.partial(nudge_kernel, stages), 'nudge', shape((kinds, tile...]
  transfers between devices with their start and end apart: 5 -> 5, of which waited for: 1 -> 3; matrix products, arithmetic and copies ran while one was open for 0% -> 0% of each run, Pallas kernels for 24% -> 14%
where the time goes in v1:
time: 44.5 us; the launch traced here: 44.2 us
  Pallas kernels  26.1 us (59%)
  starting transfers between devices  11.6 us (26%)
  waiting for transfers between devices  5.44 us (12%)
  local copies, waits for them, and re-layouts  0.74 us (2%)
    pallas_call x1, Pallas kernels, local(): call(functools.partial(sums_kernel, cap), 'column_sums', (shape((WORDS, s...  8.85 us
    pallas_call x1, Pallas kernels, local(): call(functools.partial(nudge_kernel, stages), 'nudge', shape((kinds, tile...  8.47 us
    pallas_call x1, Pallas kernels, local(): call(stencil_kernel, 'stencil', (shape(model_state.shape, f32), shape((2,...  6.16 us
    all_to_all x1, starting transfers between devices, local(): lax.all_to_all(msg, ('gx', 'gy'), split_axis=0, concat_axis=0, tiled=True)  6.05 us
    ppermute x1, starting transfers between devices, local(): lax.ppermute(give_b, 'gy', [(i, (i - 1 ^ 1) + 1) for i in range(1, count_...  3.41 us
    ppermute x1, waiting for transfers between devices, local(): lax.ppermute(give_b, 'gy', [(i, (i - 1 ^ 1) + 1) for i in range(1, count_...  3.31 us
    pallas_call x1, Pallas kernels, local(): call(functools.partial(pack_kernel, count_y, cap), 'pack_records', (shape...  2.57 us
    ppermute x1, starting transfers between devices, local(): got_a = lax.ppermute(give_a, 'gy', [(i, i ^ 1) for i in range(count_y)])  1.53 us
  transfers between devices with their start and end apart: 5, of which 3 were waited for; matrix products, arithmetic and copies ran while one was open for 0% of the time, Pallas kernels for 14%

profile of v1, /device:TPU:8, one launch (start us, length us, event | category | flops | bytes accessed | tf_op | source)
XLA Modules:
  0.0 44.2 jit_solution(2778573806801034552)
XLA Ops:
  0.0 2.6 %pack_records.1 = (f32[32,8,128]{2,1,0:T(8,128)}, f32[24,24]{1,0:T(8,128)}) custom-call(s32[1,128]{1,0:T(1,128)} %bitcast.9, s32[1,128]{1,0:T(1,128)} %bitcast.10, s32[1,128]{1,0:T(1,128)} %bitcast.11, f32[128,384]{1,0:T(8,128)} %refs_3_.1, f32[24,128]{1,0:T(8,128)} %bitcast.8), custom_call_target="tpu_custom_call" | custom-call | flops 10000000 | bytes 1000000 | tf_op jit(solution)/shard_map/pack_records/pallas_call | solution.py:400
  2.6 6.0 %all-to-all-start = ((f32[32,8,128]{2,1,0:T(8,128)}), f32[32,8,128]{2,1,0:T(8,128)S(1)}, u32[]{:S(2)}, u32[]{:S(2)}) async-start(f32[32,8,128]{2,1,0:T(8,128)} %get-tuple-element.16), calls=%async_computation | async-start | bytes 262144 | tf_op jit(solution)/shard_map/all_to_all | solution.py:422
  8.6 6.2 %stencil.1 = (f32[3,8,384,128]{3,2,1,0:T(8,128)}, f32[2,24,128]{2,1,0:T(8,128)}) custom-call(f32[3,8,384,128]{3,2,1,0:T(8,128)} %state_hbm.1), custom_call_target="tpu_custom_call" | custom-call | bytes 10000000 | tf_op jit(solution)/shard_map/stencil/pallas_call | solution.py:424
  14.8 0.8 %all-to-all-done.recv_ref = f32[32,8,128]{2,1,0:T(8,128)S(1)} async-done(((f32[32,8,128]{2,1,0:T(8,128)}), f32[32,8,128]{2,1,0:T(8,128)S(1)}, u32[]{:S(2)}, u32[]{:S(2)}) %all-to-all-start) | async-done | bytes 131104 | tf_op jit(solution)/shard_map/all_to_all | solution.py:422
  15.6 0.0 copy-start
  15.6 0.7 %copy-done = f32[2,24,128]{2,1,0:T(8,128)S(1)} copy-done((f32[2,24,128]{2,1,0:T(8,128)S(1)}, f32[2,24,128]{2,1,0:T(8,128)}, u32[]{:S(2)}) %copy-start) | copy-done | bytes 24600
  16.4 0.0 copy-start.1
  16.4 8.9 %column_sums.1 = (f32[32,1024]{1,0:T(8,128)S(1)}, bf16[768,1024]{1,0:T(8,128)(2,1)S(1)}, f32[8,1024]{1,0:T(8,128)S(1)}, f32[24,1024]{1,0:T(8,128)S(1)}, s32[8]{0...) custom-call(f32[32,8,128]{2,1,0:T(8,128)S(1)} %all-to-all-done.recv_ref, f32[2,24,128]{2,1,0:T(8,128)S(1)} %copy-done, ...), custom_call_target="tpu_custom_call" | custom-call | flops 4000000000 | bytes 10000000 | tf_op jit(solution)/shard_map/column_sums/pallas_call | solution.py:441
  25.2 0.1 collective-permute-start
  25.3 1.3 %collective-permute-done.refs_1_ = f32[32,1024]{1,0:T(8,128)S(1)} collective-permute-done((f32[32,1024]{1,0:T(8,128)S(1)}, f32[32,1024]{1,0:T(8,128)S(1)}, u32[]{:S(2)}, u32[]{:S(2)}) %collective-permute-start) | collective-permute-done | bytes 131104 | tf_op jit(solution)/shard_map/ppermute | solution.py:478
  26.6 0.1 add_select_fusion.refs_0_
  26.7 0.5 %collective-permute-start.1 = (f32[32,1024]{1,0:T(8,128)S(1)}, f32[32,1024]{1,0:T(8,128)S(1)}, u32[]{:S(2)}, u32[]{:S(2)}) collective-permute-start(f32[32,1024]{1,0:T(8,128)S(1)} %add_select_fusion.refs_0_), channel_id=1, source_target_pairs={{0,24},{8,16},{16,8},{24,0},{1,25},{9,17},{17,9},{25,1},{2,26},{10... | collective-permute-start | bytes 393224 | tf_op jit(solution)/shard_map/ppermute | solution.py:478
  27.2 1.5 %collective-permute-start.2 = (f32[24,384]{1,0:T(8,128)S(1)}, f32[24,384]{1,0:T(8,128)S(1)}, u32[]{:S(2)}, u32[]{:S(2)}) collective-permute-start(f32[24,384]{1,0:T(8,128)S(1)} %get-tuple-element.24.refs_7_), channel_id=1, source_target_pairs={{0,1},{1,0},{2,3},{3,2},{4,5},{5,4},{6,7},{7,6},{8,9},{9,8},{10,11... | collective-permute-start | bytes 110600 | tf_op jit(solution)/shard_map/ppermute | solution.py:471
  28.8 3.4 %collective-permute-start.3 = (f32[24,384]{1,0:T(8,128)S(1)}, f32[24,384]{1,0:T(8,128)S(1)}, u32[]{:S(2)}, u32[]{:S(2)}) collective-permute-start(f32[24,384]{1,0:T(8,128)S(1)} %get-tuple-element.25.refs_8_), channel_id=1, source_target_pairs={{1,2},{2,1},{3,4},{4,3},{5,6},{6,5},{9,10},{10,9},{11,12},{12,11},... | collective-permute-start | bytes 110600 | tf_op jit(solution)/shard_map/ppermute | solution.py:472
  32.2 0.0 collective-permute-done.2.refs_9_
  32.2 3.3 %collective-permute-done.3.refs_10_ = f32[24,384]{1,0:T(8,128)S(1)} collective-permute-done((f32[24,384]{1,0:T(8,128)S(1)}, f32[24,384]{1,0:T(8,128)S(1)}, u32[]{:S(2)}, u32[]{:S(2)}) %collective-permute-start.3) | collective-permute-done | bytes 36896 | tf_op jit(solution)/shard_map/ppermute | solution.py:472
  35.5 0.0 collective-permute-done.1.refs_2_
  35.5 0.0 copy-done.1
  35.5 8.5 %nudge.1 = f32[24,384,128]{2,1,0:T(8,128)} custom-call(s32[8]{0:T(128)S(1)} %get-tuple-element.18.bounds_ref, f32[32,1024]{1,0:T(8,128)S(1)} %add_select_fusion.refs_0_, f32[32,1024]{1,0:T(8,128)S(1)} %collective-permute-done.refs_1_, f32[32,1024]{1,0:T(8,128)S(1)} %collective-permute-done.1.refs_2_, f32[24,1024]{1,0:T(8,128)S(1)} %get-tuple-element.20.refs_3_, ...), custom_call_target="tpu_custom_call" | custom-call | flops 4000000000 | bytes 10000000 | tf_op jit(solution)/shard_map/nudge/pallas_call | solution.py:483
  (1 shorter events, 0.0 us)
Async XLA Ops:
  2.6 13.0 %all-to-all-start = ((f32[32,8,128]{2,1,0:T(8,128)}), f32[32,8,128]{2,1,0:T(8,128)S(1)}, u32[]{:S(2)}, u32[]{:S(2)}) async-start(f32[32,8,128]{2,1,0:T(8,128)} %get-tuple-element.16), calls=%async_computation | async-start | bytes 262144 | tf_op jit(solution)/shard_map/all_to_all | solution.py:422
  15.6 0.7 %copy-start = (f32[2,24,128]{2,1,0:T(8,128)S(1)}, f32[2,24,128]{2,1,0:T(8,128)}, u32[]{:S(2)}) copy-start(f32[2,24,128]{2,1,0:T(8,128)} %get-tuple-element.17.edge_hbm) | copy-start | bytes 73732
  16.4 19.2 %copy-start.1 = (f32[24,24]{1,0:T(8,128)S(1)}, f32[24,24]{1,0:T(8,128)}, u32[]{:S(2)}) copy-start(f32[24,24]{1,0:T(8,128)} %get-tuple-element.21.refs_4_) | copy-start | bytes 6916
  25.2 1.4 %collective-permute-start = (f32[32,1024]{1,0:T(8,128)S(1)}, f32[32,1024]{1,0:T(8,128)S(1)}, u32[]{:S(2)}, u32[]{:S(2)}) collective-permute-start(f32[32,1024]{1,0:T(8,128)S(1)} %get-tuple-element.19), channel_id=1, source_target_pairs={{0,8},{8,0},{16,24},{24,16},{1,9},{9,1},{17,25},{25,17},{2,10},{10... | collective-permute-start | bytes 393224 | tf_op jit(solution)/shard_map/ppermute | solution.py:478
  26.7 8.8 %collective-permute-start.1 = (f32[32,1024]{1,0:T(8,128)S(1)}, f32[32,1024]{1,0:T(8,128)S(1)}, u32[]{:S(2)}, u32[]{:S(2)}) collective-permute-start(f32[32,1024]{1,0:T(8,128)S(1)} %add_select_fusion.refs_0_), channel_id=1, source_target_pairs={{0,24},{8,16},{16,8},{24,0},{1,25},{9,17},{17,9},{25,1},{2,26},{10... | collective-permute-start | bytes 393224 | tf_op jit(solution)/shard_map/ppermute | solution.py:478
  27.2 5.0 %collective-permute-start.2 = (f32[24,384]{1,0:T(8,128)S(1)}, f32[24,384]{1,0:T(8,128)S(1)}, u32[]{:S(2)}, u32[]{:S(2)}) collective-permute-start(f32[24,384]{1,0:T(8,128)S(1)} %get-tuple-element.24.refs_7_), channel_id=1, source_target_pairs={{0,1},{1,0},{2,3},{3,2},{4,5},{5,4},{6,7},{7,6},{8,9},{9,8},{10,11... | collective-permute-start | bytes 110600 | tf_op jit(solution)/shard_map/ppermute | solution.py:471
  28.8 6.7 %collective-permute-start.3 = (f32[24,384]{1,0:T(8,128)S(1)}, f32[24,384]{1,0:T(8,128)S(1)}, u32[]{:S(2)}, u32[]{:S(2)}) collective-permute-start(f32[24,384]{1,0:T(8,128)S(1)} %get-tuple-element.25.refs_8_), channel_id=1, source_target_pairs={{1,2},{2,1},{3,4},{4,3},{5,6},{6,5},{9,10},{10,9},{11,12},{12,11},... | collective-permute-start | bytes 110600 | tf_op jit(solution)/shard_map/ppermute | solution.py:472

commit v2 on v1

--- a/solution.py
+++ b/solution.py
@@ -18,6 +18,7 @@
 WORDS = 32
 LANE_STEP = 32
 YB = 16
+PARTS = 4
 RB = 256
 MIB = 1024 * 1024
 MOST = 58
@@ -44,6 +45,18 @@
 
 def iota(shape, axis):
     return lax.broadcasted_iota(jnp.int32, shape, axis)
+
+
+def each(count, action):
+    lax.fori_loop(0, count, lambda i, carry: (action(i), carry)[1], 0)
+
+
+def part_copies(source, target, sem, size):
+    def copy(i):
+        some = pl.ds(pl.multiple_of(i * size, size), size)
+        return pltpu.make_async_copy(source.at[some], target.at[some], sem.at[i])
+
+    return copy
 
 
 def pack_kernel(count_y, cap, *refs):
@@ -132,25 +145,21 @@
 def edge_place(slots, k, side):
     per = slots // LANES
     rows = -(-24 // per)
-    return 25 + side * rows + k // per, (k % per) * LANES
+    return pl.ds(25 + side * rows + k // per, 1), pl.ds((k % per) * LANES, LANES)
 
 
 def sums_kernel(
-    cap, recv_ref, edge_hbm, state_hbm, cress_hbm,
+    cap, recv_ref, base_hbm, state_hbm, cress_hbm,
     msg_ref, wt_ref, ys_ref, terms_ref, bounds_ref, give_a_ref, give_b_ref,
-    acc_ref, edge_ref, state, cress, mt_hi, mt_lo, ct, sems, edge_sem,
+    acc_ref, state, cress, mt_hi, mt_lo, ct, cress_sems, state_sems,
 ):
     kinds, tile_x, tile_y = state.shape
     width = cress.shape[0]
     blocks = recv_ref.shape[0] * cap // RB
-    piece, planes = width // blocks, kinds // blocks
-    cress_reads, state_reads = [], []
-    for i in range(blocks):
-        rows, some = pl.ds(i * piece, piece), pl.ds(i * planes, planes)
-        cress_reads.append(pltpu.make_async_copy(cress_hbm.at[rows], cress.at[rows], sems.at[i]))
-        state_reads.append(pltpu.make_async_copy(state_hbm.at[some], state.at[some], sems.at[blocks + i]))
-    for read in cress_reads:
-        read.start()
+    cress_read = part_copies(cress_hbm, cress, cress_sems, width // PARTS)
+    state_read = part_copies(state_hbm, state, state_sems, kinds // PARTS)
+    each(PARTS, lambda i: cress_read(i).start())
+    each(PARTS, lambda i: state_read(i).start())
     slots = recv_ref.shape[0] * cap
     chunks = slots // LANES
 
@@ -186,11 +195,7 @@
     low = words - high - middle
     table = jnp.concatenate([top, high, middle, low], axis=0).astype(jnp.bfloat16)
 
-    for read in state_reads:
-        read.start()
     even = lax.rem(lax.axis_index("gy"), 2) == 0
-    edge_read = pltpu.make_async_copy(edge_hbm, edge_ref, edge_sem)
-    edge_read.start()
     x_rows = []
     for j in range(blocks):
         lanes = slice(j * RB, (j + 1) * RB)
@@ -206,8 +211,7 @@
         bounds_ref[2 * j] = least // YB
         bounds_ref[2 * j + 1] = most // YB + 1
 
-    for read in cress_reads:
-        read.wait()
+    each(PARTS, lambda i: cress_read(i).wait())
     for i in range(width // LANES):
         rows = slice(i * LANES, (i + 1) * LANES)
         high, low = split2(jnp.transpose(cress[rows, :]))
@@ -222,8 +226,7 @@
     half = blocks // 2
     for j in range(half):
         gather(j)
-    for read in state_reads:
-        read.wait()
+    each(PARTS, lambda i: state_read(i).wait())
     planes = kinds // (blocks - half)
     for j in range(half, blocks):
         gather(j)
@@ -256,33 +259,34 @@
         total = dot(ones, wt_ref[:, lanes])
         msg_ref[kinds : kinds + 1, lanes] = total[0:1]
     msg_ref[kinds + 1 :, :] = jnp.zeros((WORDS - kinds - 1, slots), jnp.float32)
-    edge_read.wait()
-    for side in range(2):
+    for side, edge in enumerate((0, tile_x - 1)):
         for k in range(kinds):
-            r, at = edge_place(slots, k, side)
-            msg_ref[r : r + 1, at : at + LANES] = edge_ref[side, k : k + 1, :]
-
-
-def stencil_kernel(state_hbm, out_hbm, edge_ref, state, out, sems, out_sems):
+            msg_ref[edge_place(slots, k, side)] = state[k, edge : edge + 1, :]
+
+
+def stencil_kernel(state_hbm, out_hbm, state, out, in_sems, out_sems):
     fields, levels, tile_x, tile_y = state.shape
-    reads = [
-        pltpu.make_async_copy(state_hbm.at[:, z], state.at[:, z], sems.at[z]) for z in range(levels)
-    ]
-    writes = [
-        pltpu.make_async_copy(out.at[:, z], out_hbm.at[:, z], out_sems.at[z]) for z in range(levels)
-    ]
-    for read in reads:
-        read.start()
-    reads[0].wait()
+
+    def read(z):
+        return pltpu.make_async_copy(state_hbm.at[:, z], state.at[:, z], in_sems.at[z])
+
+    def write(z):
+        return pltpu.make_async_copy(out.at[:, z], out_hbm.at[:, z], out_sems.at[z])
+
+    each(levels, lambda z: read(z).start())
+    read(0).wait()
     row = iota((tile_x, tile_y), 0)
     lane = iota((tile_x, tile_y), 1)
     wind = 0.5 * time_step * advect_coef
     across = time_step * diffuse_h
     upward = time_step * diffuse_z
     keep = 1.0 - 4.0 * across - 2.0 * upward
-    for z in range(levels):
-        if z + 1 < levels:
-            reads[z + 1].wait()
+
+    def level(z):
+        @pl.when(z + 1 < levels)
+        def _():
+            read(z + 1).wait()
+
         u = wind * state[0, z]
         v = wind * state[1, z]
         east_gain = jnp.where(row == tile_x - 1, 0.0, across - u)
@@ -291,18 +295,17 @@
         south_gain = jnp.where(lane == 0, 0.0, across + v)
         for f in range(fields):
             cell = state[f, z]
-            edge_ref[0, f * levels + z : f * levels + z + 1, :] = cell[0:1]
-            edge_ref[1, f * levels + z : f * levels + z + 1, :] = cell[tile_x - 1 :]
-            stacked = state[f, min(z + 1, levels - 1)] + state[f, max(z - 1, 0)]
+            stacked = state[f, jnp.minimum(z + 1, levels - 1)] + state[f, jnp.maximum(z - 1, 0)]
             total = keep * cell + upward * stacked
             total = total + east_gain * pltpu.roll(cell, tile_x - 1, 0)
             total = total + west_gain * pltpu.roll(cell, 1, 0)
             total = total + north_gain * pltpu.roll(cell, tile_y - 1, 1)
             total = total + south_gain * pltpu.roll(cell, 1, 1)
             out[f, z] = total
-        writes[z].start()
-    for write in writes:
-        write.wait()
+        write(z).start()
+
+    each(levels, level)
+    each(levels, lambda z: write(z).wait())
 
 
 def nudge_kernel(stages, bounds_ref, *refs):
@@ -310,13 +313,13 @@
     even = lax.rem(lax.axis_index("gy"), 2) == 0
     sum_ref, recv_refs, refs = refs[0], refs[1 : 1 + stages], refs[1 + stages :]
     (terms_ref, gram_ref, ys_ref, wt_ref, give_a, give_b, got_a, got_b,
-     base_hbm, out_hbm, num_ref, base, out, spread_ref, in_sem, out_sems) = refs
+     base_hbm, out_hbm, num_ref, base, out, spread_ref, y_add, x_add, in_sems, out_sems) = refs
     kinds, tile_x, tile_y = base.shape
     levels = kinds // 3
     slots = ys_ref.shape[1]
     blocks = slots // RB
-    read = pltpu.make_async_copy(base_hbm, base, in_sem)
-    read.start()
+    read = part_copies(base_hbm, base, in_sems, kinds // PARTS)
+    each(PARTS, lambda i: read(i).start())
     num_ref[...] = jnp.zeros_like(num_ref)
     total = sum_ref[0 : kinds + 1, :] + recv_refs[-1][0 : kinds + 1, :]
     averaged = total[0:kinds] / total[kinds : kinds + 1]
@@ -338,36 +341,41 @@
     wind = 0.5 * time_step * advect_coef
     across = time_step * diffuse_h
     scale = time_step * nudge_gain / jnp.maximum(num_ref[kinds], 1.0)
-    read.wait()
+    v_rows = slice(levels, 2 * levels)
+    v_a = jnp.concatenate([give_a[v_rows, :]] * 3, axis=0)
+    v_b = jnp.concatenate([give_b[v_rows, :]] * 3, axis=0)
+    north = jnp.where(even, got_a[...], got_b[...]) * (across - wind * jnp.where(even, v_a, v_b))
+    south = jnp.where(even, got_b[...], got_a[...]) * (across + wind * jnp.where(even, v_b, v_a))
     for k in range(kinds):
-        z = k % levels
-        turned = num_ref[k] * scale
-        v_row = slice(levels + z, levels + z + 1)
-        beyond_a, beyond_b = got_a[k : k + 1, :], got_b[k : k + 1, :]
-        v_a, v_b = give_a[v_row, :], give_b[v_row, :]
-        north = jnp.where(even, beyond_a, beyond_b) * (across - wind * jnp.where(even, v_a, v_b))
-        south = jnp.where(even, beyond_b, beyond_a) * (across + wind * jnp.where(even, v_b, v_a))
-        cell_row = iota(turned.shape, 0)
-        turned = turned + jnp.where(
-            cell_row == 0, south, jnp.where(cell_row == tile_y - 1, north, 0.0)
-        )
-        out[k] = base[k] + jnp.transpose(turned)
+        y_add[k, 0:1, :] = south[k : k + 1, :]
+        y_add[k, 1:2, :] = north[k : k + 1, :]
         west = jnp.zeros((1, tile_y), jnp.float32)
         east = jnp.zeros((1, tile_y), jnp.float32)
         for s in range(stages):
-            r, at = edge_place(slots, k, 1)
-            west = west + jnp.where(me ^ (2 ** (s + 1) - 1) == me - 1, recv_refs[s][r : r + 1, at : at + LANES], 0.0)
-            r, at = edge_place(slots, k, 0)
-            east = east + jnp.where(me ^ (2 ** (s + 1) - 1) == me + 1, recv_refs[s][r : r + 1, at : at + LANES], 0.0)
-        r, at = edge_place(slots, z, 0)
-        u_first = sum_ref[r : r + 1, at : at + LANES]
-        r, at = edge_place(slots, z, 1)
-        u_last = sum_ref[r : r + 1, at : at + LANES]
-        out[k, 0:1, :] += west * (across + wind * u_first)
-        out[k, tile_x - 1 : tile_x, :] += east * (across - wind * u_last)
+            partner = me ^ (2 ** (s + 1) - 1)
+            west = west + jnp.where(partner == me - 1, recv_refs[s][edge_place(slots, k, 1)], 0.0)
+            east = east + jnp.where(partner == me + 1, recv_refs[s][edge_place(slots, k, 0)], 0.0)
+        z = k % levels
+        x_add[k, 0:1, :] = west * (across + wind * sum_ref[edge_place(slots, z, 0)])
+        x_add[k, 1:2, :] = east * (across - wind * sum_ref[edge_place(slots, z, 1)])
+    each(PARTS, lambda i: read(i).wait())
+    cell_row = iota((tile_y, tile_x), 0)
+
+    def finish(k):
+        edges = jnp.where(
+            cell_row == 0, y_add[k, 0:1, :], jnp.where(cell_row == tile_y - 1, y_add[k, 1:2, :], 0.0)
+        )
+        out[k] = base[k] + jnp.transpose(num_ref[k] * scale + edges)
+        out[k, 0:1, :] += x_add[k, 0:1, :]
+        out[k, tile_x - 1 : tile_x, :] += x_add[k, 1:2, :]
         pltpu.make_async_copy(out.at[k], out_hbm.at[k], out_sems.at[k]).start()
-    for k in range(kinds):
-        pltpu.make_async_copy(out.at[k], out_hbm.at[k], out_sems.at[k]).wait()
+
+    def finish_some(i):
+        for n in range(levels):
+            finish(i * levels + n)
+
+    each(kinds // levels, finish_some)
+    each(kinds, lambda k: pltpu.make_async_copy(out.at[k], out_hbm.at[k], out_sems.at[k]).wait())
 
 
 def call(kernel, name, out_shape, in_specs, out_specs, scratch=(), vmem=8, flops=0, moved=0):
@@ -421,12 +429,12 @@
     )
     recv = lax.all_to_all(msg, ("gx", "gy"), split_axis=0, concat_axis=0, tiled=True)
 
-    base, edges = call(
+    base = call(
         stencil_kernel,
         "stencil",
-        (shape(model_state.shape, f32), shape((2, kinds, tile_y), f32)),
+        shape(model_state.shape, f32),
         [HBM],
-        (HBM, VMEM),
+        HBM,
         [
             pltpu.VMEM(model_state.shape, f32),
             pltpu.VMEM(model_state.shape, f32),
@@ -454,19 +462,18 @@
         (VMEM, VMEM, VMEM, VMEM, SMEM, VMEM, VMEM),
         [
             pltpu.VMEM((blocks, kinds, 8, RB), f32),
-            pltpu.VMEM((2, kinds, tile_y), f32),
             pltpu.VMEM((kinds, tile_x, tile_y), f32),
             pltpu.VMEM((width, tile_x), f32),
             pltpu.VMEM((kinds, tile_y, tile_x), bf16),
             pltpu.VMEM((kinds, tile_y, tile_x), bf16),
             pltpu.VMEM((2 * tile_x, width), bf16),
-            pltpu.SemaphoreType.DMA((2 * blocks,)),
-            pltpu.SemaphoreType.DMA,
+            pltpu.SemaphoreType.DMA((PARTS,)),
+            pltpu.SemaphoreType.DMA((PARTS,)),
         ],
         vmem=SOME,
         flops=4 * 10**9,
         moved=10**7,
-    )(recv, edges, state3, cressman)
+    )(recv, base, state3, cressman)
 
     got_a = lax.ppermute(give_a, "gy", [(i, i ^ 1) for i in range(count_y)])
     got_b = lax.ppermute(give_b, "gy", [(i, ((i - 1) ^ 1) + 1) for i in range(1, count_y - 1)])
@@ -491,7 +498,9 @@
             pltpu.VMEM((kinds, tile_x, tile_y), f32),
             pltpu.VMEM((kinds, tile_x, tile_y), f32),
             pltpu.VMEM((WORDS, slots), f32),
-            pltpu.SemaphoreType.DMA,
+            pltpu.VMEM((kinds, 2, tile_x), f32),
+            pltpu.VMEM((kinds, 2, tile_y), f32),
+            pltpu.SemaphoreType.DMA((PARTS,)),
             pltpu.SemaphoreType.DMA((kinds,)),
         ],
         vmem=SOME,

time: 44.5 us -> 41.4 us (0.930)
  Pallas kernels: 26.1 us -> 23.4 us
  local copies, waits for them, and re-layouts: 0.74 us -> 0.01 us
    pallas_call x1, Pallas kernels: 8.47 us -> 6.92 us  [local(): call(functools.partial(nudge_kernel, stages), 'nudge', shape((kinds, tile...]
    unnamed x4 -> x2, local copies, waits for them, and re-layouts: 0.74 us -> 0.01 us
    ppermute x1, starting transfers between devices: 1.53 us -> 0.9 us  [local(): got_a = lax.ppermute(give_a, 'gy', [(i, i ^ 1) for i in range(count_y)])]
    pallas_call x1, Pallas kernels: 8.85 us -> 8.27 us  [local(): call(functools.partial(sums_kernel, cap), 'column_sums', (shape((WORDS, s...]
    all_to_all x1, waiting for transfers between devices: 0.81 us -> 1.36 us  [local(): lax.all_to_all(msg, ('gx', 'gy'), split_axis=0, concat_axis=0, tiled=True)]
    pallas_call x1, Pallas kernels: 6.16 us -> 5.62 us  [local(): call(stencil_kernel, 'stencil', shape(model_state.shape, f32), [HBM], HBM...]
    ppermute x1, starting transfers between devices: 3.41 us -> 3.95 us  [local(): lax.ppermute(give_b, 'gy', [(i, (i - 1 ^ 1) + 1) for i in range(1, count_...]
    ppermute x1, waiting for transfers between devices: 3.31 us -> 2.77 us  [local(): lax.ppermute(give_b, 'gy', [(i, (i - 1 ^ 1) + 1) for i in range(1, count_...]
where the time goes in v2:
time: 41.4 us; the launch traced here: 40.7 us
  Pallas kernels  23.4 us (57%)
  starting transfers between devices  11.5 us (28%)
  waiting for transfers between devices  5.45 us (13%)
    pallas_call x1, Pallas kernels, local(): call(functools.partial(sums_kernel, cap), 'column_sums', (shape((WORDS, s...  8.27 us
    pallas_call x1, Pallas kernels, local(): call(functools.partial(nudge_kernel, stages), 'nudge', shape((kinds, tile...  6.92 us
    all_to_all x1, starting transfers between devices, local(): lax.all_to_all(msg, ('gx', 'gy'), split_axis=0, concat_axis=0, tiled=True)  6.05 us
    pallas_call x1, Pallas kernels, local(): call(stencil_kernel, 'stencil', shape(model_state.shape, f32), [HBM], HBM...  5.62 us
    ppermute x1, starting transfers between devices, local(): lax.ppermute(give_b, 'gy', [(i, (i - 1 ^ 1) + 1) for i in range(1, count_...  3.95 us
    ppermute x1, waiting for transfers between devices, local(): lax.ppermute(give_b, 'gy', [(i, (i - 1 ^ 1) + 1) for i in range(1, count_...  2.77 us
    pallas_call x1, Pallas kernels, local(): call(functools.partial(pack_kernel, count_y, cap), 'pack_records', (shape...  2.57 us
    all_to_all x1, waiting for transfers between devices, local(): lax.all_to_all(msg, ('gx', 'gy'), split_axis=0, concat_axis=0, tiled=True)  1.36 us
  transfers between devices with their start and end apart: 5, of which 3 were waited for; matrix products, arithmetic and copies ran while one was open for 0% of the time, Pallas kernels for 14%

profile of v2, /device:TPU:8, one launch (start us, length us, event | category | flops | bytes accessed | tf_op | source)
XLA Modules:
  0.0 40.7 jit_solution(5689239399071000113)
XLA Ops:
  0.0 2.6 %pack_records.1 = (f32[32,8,128]{2,1,0:T(8,128)}, f32[24,24]{1,0:T(8,128)}) custom-call(s32[1,128]{1,0:T(1,128)} %bitcast.10, s32[1,128]{1,0:T(1,128)} %bitcast.11, s32[1,128]{1,0:T(1,128)} %bitcast.12, f32[128,384]{1,0:T(8,128)} %refs_3_.1, f32[24,128]{1,0:T(8,128)} %bitcast.9), custom_call_target="tpu_custom_call" | custom-call | flops 10000000 | bytes 1000000 | tf_op jit(solution)/shard_map/pack_records/pallas_call | solution.py:408
  2.6 6.0 %all-to-all-start = ((f32[32,8,128]{2,1,0:T(8,128)}), f32[32,8,128]{2,1,0:T(8,128)S(1)}, u32[]{:S(2)}, u32[]{:S(2)}) async-start(f32[32,8,128]{2,1,0:T(8,128)} %get-tuple-element.14), calls=%async_computation | async-start | bytes 262144 | tf_op jit(solution)/shard_map/all_to_all | solution.py:430
  8.6 5.6 %stencil.1.base_hbm = f32[3,8,384,128]{3,2,1,0:T(8,128)} custom-call(f32[3,8,384,128]{3,2,1,0:T(8,128)} %state_hbm.1), custom_call_target="tpu_custom_call" | custom-call | bytes 10000000 | tf_op jit(solution)/shard_map/stencil/pallas_call | solution.py:432
  14.3 1.4 %all-to-all-done.recv_ref = f32[32,8,128]{2,1,0:T(8,128)S(1)} async-done(((f32[32,8,128]{2,1,0:T(8,128)}), f32[32,8,128]{2,1,0:T(8,128)S(1)}, u32[]{:S(2)}, u32[]{:S(2)}) %all-to-all-start) | async-done | bytes 131104 | tf_op jit(solution)/shard_map/all_to_all | solution.py:430
  15.6 0.0 copy-start
  15.6 8.3 %column_sums.1 = (f32[32,1024]{1,0:T(8,128)S(1)}, bf16[768,1024]{1,0:T(8,128)(2,1)S(1)}, f32[8,1024]{1,0:T(8,128)S(1)}, f32[24,1024]{1,0:T(8,128)S(1)}, s32[8]{0...) custom-call(f32[32,8,128]{2,1,0:T(8,128)S(1)} %all-to-all-done.recv_ref, f32[3,8,384,128]{3,2,1,0:T(8,128)} %stencil.1.base_hbm, ...), custom_call_target="tpu_custom_call" | custom-call | flops 4000000000 | bytes 10000000 | tf_op jit(solution)/shard_map/column_sums/pallas_call | solution.py:449
  23.9 0.1 collective-permute-start
  24.0 1.3 %collective-permute-done.refs_1_ = f32[32,1024]{1,0:T(8,128)S(1)} collective-permute-done((f32[32,1024]{1,0:T(8,128)S(1)}, f32[32,1024]{1,0:T(8,128)S(1)}, u32[]{:S(2)}, u32[]{:S(2)}) %collective-permute-start) | collective-permute-done | bytes 131104 | tf_op jit(solution)/shard_map/ppermute | solution.py:485
  25.3 0.1 add_select_fusion.refs_0_
  25.4 0.5 %collective-permute-start.1 = (f32[32,1024]{1,0:T(8,128)S(1)}, f32[32,1024]{1,0:T(8,128)S(1)}, u32[]{:S(2)}, u32[]{:S(2)}) collective-permute-start(f32[32,1024]{1,0:T(8,128)S(1)} %add_select_fusion.refs_0_), channel_id=1, source_target_pairs={{0,24},{8,16},{16,8},{24,0},{1,25},{9,17},{17,9},{25,1},{2,26},{10... | collective-permute-start | bytes 393224 | tf_op jit(solution)/shard_map/ppermute | solution.py:485
  25.9 0.9 %collective-permute-start.2 = (f32[24,384]{1,0:T(8,128)S(1)}, f32[24,384]{1,0:T(8,128)S(1)}, u32[]{:S(2)}, u32[]{:S(2)}) collective-permute-start(f32[24,384]{1,0:T(8,128)S(1)} %get-tuple-element.21.refs_7_), channel_id=1, source_target_pairs={{0,1},{1,0},{2,3},{3,2},{4,5},{5,4},{6,7},{7,6},{8,9},{9,8},{10,11... | collective-permute-start | bytes 110600 | tf_op jit(solution)/shard_map/ppermute | solution.py:478
  26.8 4.0 %collective-permute-start.3 = (f32[24,384]{1,0:T(8,128)S(1)}, f32[24,384]{1,0:T(8,128)S(1)}, u32[]{:S(2)}, u32[]{:S(2)}) collective-permute-start(f32[24,384]{1,0:T(8,128)S(1)} %get-tuple-element.22.refs_8_), channel_id=1, source_target_pairs={{1,2},{2,1},{3,4},{4,3},{5,6},{6,5},{9,10},{10,9},{11,12},{12,11},... | collective-permute-start | bytes 110600 | tf_op jit(solution)/shard_map/ppermute | solution.py:479
  30.8 0.0 collective-permute-done.2.refs_9_
  30.8 2.8 %collective-permute-done.3.refs_10_ = f32[24,384]{1,0:T(8,128)S(1)} collective-permute-done((f32[24,384]{1,0:T(8,128)S(1)}, f32[24,384]{1,0:T(8,128)S(1)}, u32[]{:S(2)}, u32[]{:S(2)}) %collective-permute-start.3) | collective-permute-done | bytes 36896 | tf_op jit(solution)/shard_map/ppermute | solution.py:479
  33.6 0.0 collective-permute-done.1.refs_2_
  33.6 0.0 copy-done
  33.6 6.9 %nudge.1 = f32[24,384,128]{2,1,0:T(8,128)} custom-call(s32[8]{0:T(128)S(1)} %get-tuple-element.15.bounds_ref, f32[32,1024]{1,0:T(8,128)S(1)} %add_select_fusion.refs_0_, f32[32,1024]{1,0:T(8,128)S(1)} %collective-permute-done.refs_1_, f32[32,1024]{1,0:T(8,128)S(1)} %collective-permute-done.1.refs_2_, f32[24,1024]{1,0:T(8,128)S(1)} %get-tuple-element.17.refs_3_, ...), custom_call_target="tpu_custom_call" | custom-call | flops 4000000000 | bytes 10000000 | tf_op jit(solution)/shard_map/nudge/pallas_call | solution.py:490
  (1 shorter events, 0.0 us)
Async XLA Ops:
  2.6 13.0 %all-to-all-start = ((f32[32,8,128]{2,1,0:T(8,128)}), f32[32,8,128]{2,1,0:T(8,128)S(1)}, u32[]{:S(2)}, u32[]{:S(2)}) async-start(f32[32,8,128]{2,1,0:T(8,128)} %get-tuple-element.14), calls=%async_computation | async-start | bytes 262144 | tf_op jit(solution)/shard_map/all_to_all | solution.py:430
  15.6 18.0 %copy-start = (f32[24,24]{1,0:T(8,128)S(1)}, f32[24,24]{1,0:T(8,128)}, u32[]{:S(2)}) copy-start(f32[24,24]{1,0:T(8,128)} %get-tuple-element.18.refs_4_) | copy-start | bytes 6916
  23.9 1.4 %collective-permute-start = (f32[32,1024]{1,0:T(8,128)S(1)}, f32[32,1024]{1,0:T(8,128)S(1)}, u32[]{:S(2)}, u32[]{:S(2)}) collective-permute-start(f32[32,1024]{1,0:T(8,128)S(1)} %get-tuple-element.16), channel_id=1, source_target_pairs={{0,8},{8,0},{16,24},{24,16},{1,9},{9,1},{17,25},{25,17},{2,10},{10... | collective-permute-start | bytes 393224 | tf_op jit(solution)/shard_map/ppermute | solution.py:485
  25.4 8.2 %collective-permute-start.1 = (f32[32,1024]{1,0:T(8,128)S(1)}, f32[32,1024]{1,0:T(8,128)S(1)}, u32[]{:S(2)}, u32[]{:S(2)}) collective-permute-start(f32[32,1024]{1,0:T(8,128)S(1)} %add_select_fusion.refs_0_), channel_id=1, source_target_pairs={{0,24},{8,16},{16,8},{24,0},{1,25},{9,17},{17,9},{25,1},{2,26},{10... | collective-permute-start | bytes 393224 | tf_op jit(solution)/shard_map/ppermute | solution.py:485
  25.9 4.9 %collective-permute-start.2 = (f32[24,384]{1,0:T(8,128)S(1)}, f32[24,384]{1,0:T(8,128)S(1)}, u32[]{:S(2)}, u32[]{:S(2)}) collective-permute-start(f32[24,384]{1,0:T(8,128)S(1)} %get-tuple-element.21.refs_7_), channel_id=1, source_target_pairs={{0,1},{1,0},{2,3},{3,2},{4,5},{5,4},{6,7},{7,6},{8,9},{9,8},{10,11... | collective-permute-start | bytes 110600 | tf_op jit(solution)/shard_map/ppermute | solution.py:478
  26.8 6.7 %collective-permute-start.3 = (f32[24,384]{1,0:T(8,128)S(1)}, f32[24,384]{1,0:T(8,128)S(1)}, u32[]{:S(2)}, u32[]{:S(2)}) collective-permute-start(f32[24,384]{1,0:T(8,128)S(1)} %get-tuple-element.22.refs_8_), channel_id=1, source_target_pairs={{1,2},{2,1},{3,4},{4,3},{5,6},{6,5},{9,10},{10,9},{11,12},{12,11},... | collective-permute-start | bytes 110600 | tf_op jit(solution)/shard_map/ppermute | solution.py:479

commit v3 on v2

--- a/solution.py
+++ b/solution.py
@@ -41,6 +41,13 @@
     high = value.astype(jnp.bfloat16)
     low = (value - high.astype(jnp.float32)).astype(jnp.bfloat16)
     return high, low
+
+
+def dot3(a, b, dims=NN):
+    (a_hi, a_lo), (b_hi, b_lo) = [[half.astype(jnp.float32) for half in split2(m)] for m in (a, b)]
+    a3 = jnp.concatenate([a_hi, a_hi, a_lo], axis=dims[0][0][0]).astype(jnp.bfloat16)
+    b3 = jnp.concatenate([b_hi, b_lo, b_hi], axis=dims[0][1][0]).astype(jnp.bfloat16)
+    return dot(a3, b3, dims)
 
 
 def iota(shape, axis):
@@ -73,7 +80,7 @@
     terms = []
     for v in range(3):
         obs = obs_ref[:, v * LANES : (v + 1) * LANES]
-        terms.append(dot(vert[v * levels : (v + 1) * levels], obs, NT, HIGHEST) * spread_gain)
+        terms.append(dot3(vert[v * levels : (v + 1) * levels], obs, NT) * spread_gain)
     row = iota((8, records), 0)
     x_row = jnp.broadcast_to(x_ref[...].astype(jnp.float32), (8, records))
     y_row = jnp.broadcast_to(y_ref[...].astype(jnp.float32) - float(LANES), (8, records))
@@ -89,7 +96,11 @@
     slot = owner * float(cap) + rank
     places = count_y * cap
     pick = jnp.where(iota((places, records), 0).astype(jnp.float32) == slot, 1.0, 0.0)
-    out = dot(payload, pick, NT, HIGHEST)
+    high = payload.astype(jnp.bfloat16).astype(jnp.float32)
+    middle = (payload - high).astype(jnp.bfloat16).astype(jnp.float32)
+    parts = jnp.concatenate([high, middle, payload - high - middle], axis=0).astype(jnp.bfloat16)
+    out = dot(parts, pick.astype(jnp.bfloat16), NT)
+    out = out[0:WORDS] + out[WORDS : 2 * WORDS] + out[2 * WORDS :]
 
     lane = iota((8, LANES), 1)
     for c in range(count_y):
@@ -151,7 +162,7 @@
 def sums_kernel(
     cap, recv_ref, base_hbm, state_hbm, cress_hbm,
     msg_ref, wt_ref, ys_ref, terms_ref, bounds_ref, give_a_ref, give_b_ref,
-    acc_ref, state, cress, mt_hi, mt_lo, ct, cress_sems, state_sems,
+    state, cress, mt_hi, mt_lo, ct, cress_sems, state_sems,
 ):
     kinds, tile_x, tile_y = state.shape
     width = cress.shape[0]
@@ -239,7 +250,7 @@
             give_a_ref[k : k + 1, :] = jnp.where(even, last, first)
             give_b_ref[k : k + 1, :] = jnp.where(even, first, last)
 
-    acc_ref[...] = jnp.zeros_like(acc_ref)
+    before = running = None
     y_blocks = tile_y // YB
     for j, b in pair_list(bounds_ref, blocks, y_blocks):
         lanes = pl.ds(pl.multiple_of(j * RB, RB), RB)
@@ -250,12 +261,14 @@
         part = dot(jnp.concatenate([a_hi, a_hi], axis=1), wt_ref[:, lanes]) + dot(a_lo, w_hi)
         named = (iota((YB, RB), 0) + b * YB).astype(jnp.float32) == ys_ref[0:1, lanes]
         kept = jnp.where(named[None], part.reshape(kinds, YB, RB), 0.0)
-        acc_ref[j] += kept[:, :8] + kept[:, 8:]
+        summed = jnp.sum(kept[:, :8] + kept[:, 8:], axis=1)
+        running = summed if before is None else summed + jnp.where(j == before, running, 0.0)
+        before = j
+        msg_ref[0:kinds, lanes] = running
 
     ones = jnp.ones((8, 2 * tile_x), jnp.bfloat16)
     for j in range(blocks):
         lanes = slice(j * RB, (j + 1) * RB)
-        msg_ref[0:kinds, lanes] = jnp.sum(acc_ref[j], axis=1)
         total = dot(ones, wt_ref[:, lanes])
         msg_ref[kinds : kinds + 1, lanes] = total[0:1]
     msg_ref[kinds + 1 :, :] = jnp.zeros((WORDS - kinds - 1, slots), jnp.float32)
@@ -320,13 +333,20 @@
     blocks = slots // RB
     read = part_copies(base_hbm, base, in_sems, kinds // PARTS)
     each(PARTS, lambda i: read(i).start())
-    num_ref[...] = jnp.zeros_like(num_ref)
     total = sum_ref[0 : kinds + 1, :] + recv_refs[-1][0 : kinds + 1, :]
     averaged = total[0:kinds] / total[kinds : kinds + 1]
     spread_ref[0:kinds, :] = terms_ref[...] - dot(gram_ref[...], averaged, NN, HIGHEST)
     spread_ref[kinds : kinds + 1, :] = jnp.ones((1, slots), jnp.float32)
 
     y_blocks = tile_y // YB
+    for b in range(y_blocks):
+        met = [(bounds_ref[2 * j] <= b) & (b < bounds_ref[2 * j + 1]) for j in range(blocks)]
+
+        @pl.when(jnp.logical_not(functools.reduce(jnp.logical_or, met)))
+        def _(b=b):
+            num_ref[:, b * YB : (b + 1) * YB, :] = jnp.zeros((kinds + 1, YB, tile_x), jnp.float32)
+
+    before = -1
     for j, b in pair_list(bounds_ref, blocks, y_blocks):
         lanes = pl.ds(pl.multiple_of(j * RB, RB), RB)
         start = pl.multiple_of(jnp.minimum(b, y_blocks - 1) * YB, YB)
@@ -336,7 +356,12 @@
         b_hi, b_lo = split2(placed.reshape((kinds + 1) * YB, RB))
         both = dot(b_hi, wt_ref[:, lanes], NT)
         part = both[:, 0:tile_x] + both[:, tile_x:] + dot(b_lo, wt_ref[0:tile_x, lanes], NT)
-        num_ref[:, pl.ds(start, YB), :] += part.reshape(kinds + 1, YB, tile_x)
+        fresh = (b != before) & (b < y_blocks)
+        before = b
+        rows = pl.ds(start, YB)
+        num_ref[:, rows, :] = part.reshape(kinds + 1, YB, tile_x) + jnp.where(
+            fresh, 0.0, num_ref[:, rows, :]
+        )
 
     wind = 0.5 * time_step * advect_coef
     across = time_step * diffuse_h
@@ -461,7 +486,6 @@
         [VMEM, HBM, HBM, HBM],
         (VMEM, VMEM, VMEM, VMEM, SMEM, VMEM, VMEM),
         [
-            pltpu.VMEM((blocks, kinds, 8, RB), f32),
             pltpu.VMEM((kinds, tile_x, tile_y), f32),
             pltpu.VMEM((width, tile_x), f32),
             pltpu.VMEM((kinds, tile_y, tile_x), bf16),

time: 41.4 us -> 41.1 us (level)
  no operation moved by 1% of the time
where the time goes in v3:
time: 41.1 us; the launch traced here: 40.3 us
  Pallas kernels  23 us (56%)
  starting transfers between devices  11.4 us (28%)
  waiting for transfers between devices  5.56 us (14%)
    pallas_call x1, Pallas kernels, local(): call(functools.partial(sums_kernel, cap), 'column_sums', (shape((WORDS, s...  8.27 us
    pallas_call x1, Pallas kernels, local(): call(functools.partial(nudge_kernel, stages), 'nudge', shape((kinds, tile...  6.93 us
    all_to_all x1, starting transfers between devices, local(): lax.all_to_all(msg, ('gx', 'gy'), split_axis=0, concat_axis=0, tiled=True)  6.05 us
    pallas_call x1, Pallas kernels, local(): call(stencil_kernel, 'stencil', shape(model_state.shape, f32), [HBM], HBM...  5.62 us
    ppermute x1, starting transfers between devices, local(): lax.ppermute(give_b, 'gy', [(i, (i - 1 ^ 1) + 1) for i in range(1, count_...  3.84 us
    ppermute x1, waiting for transfers between devices, local(): lax.ppermute(give_b, 'gy', [(i, (i - 1 ^ 1) + 1) for i in range(1, count_...  2.88 us
    pallas_call x1, Pallas kernels, local(): call(functools.partial(pack_kernel, count_y, cap), 'pack_records', (shape...  2.18 us
    all_to_all x1, waiting for transfers between devices, local(): lax.all_to_all(msg, ('gx', 'gy'), split_axis=0, concat_axis=0, tiled=True)  1.36 us
  transfers between devices with their start and end apart: 5, of which 3 were waited for; matrix products, arithmetic and copies ran while one was open for 0% of the time, Pallas kernels for 14%

profile of v3, /device:TPU:8, one launch (start us, length us, event | category | flops | bytes accessed | tf_op | source)
XLA Modules:
  0.0 40.3 jit_solution(10906105018755073626)
XLA Ops:
  0.0 2.2 %pack_records.1 = (f32[32,8,128]{2,1,0:T(8,128)}, f32[24,24]{1,0:T(8,128)}) custom-call(s32[1,128]{1,0:T(1,128)} %bitcast.10, s32[1,128]{1,0:T(1,128)} %bitcast.11, s32[1,128]{1,0:T(1,128)} %bitcast.12, f32[128,384]{1,0:T(8,128)} %refs_3_.1, f32[24,128]{1,0:T(8,128)} %bitcast.9), custom_call_target="tpu_custom_call" | custom-call | flops 10000000 | bytes 1000000 | tf_op jit(solution)/shard_map/pack_records/pallas_call | solution.py:433
  2.2 6.0 %all-to-all-start = ((f32[32,8,128]{2,1,0:T(8,128)}), f32[32,8,128]{2,1,0:T(8,128)S(1)}, u32[]{:S(2)}, u32[]{:S(2)}) async-start(f32[32,8,128]{2,1,0:T(8,128)} %get-tuple-element.14), calls=%async_computation | async-start | bytes 262144 | tf_op jit(solution)/shard_map/all_to_all | solution.py:455
  8.2 5.6 %stencil.1.base_hbm = f32[3,8,384,128]{3,2,1,0:T(8,128)} custom-call(f32[3,8,384,128]{3,2,1,0:T(8,128)} %state_hbm.1), custom_call_target="tpu_custom_call" | custom-call | bytes 10000000 | tf_op jit(solution)/shard_map/stencil/pallas_call | solution.py:457
  13.9 1.4 %all-to-all-done.recv_ref = f32[32,8,128]{2,1,0:T(8,128)S(1)} async-done(((f32[32,8,128]{2,1,0:T(8,128)}), f32[32,8,128]{2,1,0:T(8,128)S(1)}, u32[]{:S(2)}, u32[]{:S(2)}) %all-to-all-start) | async-done | bytes 131104 | tf_op jit(solution)/shard_map/all_to_all | solution.py:455
  15.2 0.0 copy-start
  15.2 8.3 %column_sums.1 = (f32[32,1024]{1,0:T(8,128)S(1)}, bf16[768,1024]{1,0:T(8,128)(2,1)S(1)}, f32[8,1024]{1,0:T(8,128)S(1)}, f32[24,1024]{1,0:T(8,128)S(1)}, s32[8]{0...) custom-call(f32[32,8,128]{2,1,0:T(8,128)S(1)} %all-to-all-done.recv_ref, f32[3,8,384,128]{3,2,1,0:T(8,128)} %stencil.1.base_hbm, ...), custom_call_target="tpu_custom_call" | custom-call | flops 4000000000 | bytes 10000000 | tf_op jit(solution)/shard_map/column_sums/pallas_call | solution.py:474
  23.5 0.1 collective-permute-start
  23.6 1.3 %collective-permute-done.refs_1_ = f32[32,1024]{1,0:T(8,128)S(1)} collective-permute-done((f32[32,1024]{1,0:T(8,128)S(1)}, f32[32,1024]{1,0:T(8,128)S(1)}, u32[]{:S(2)}, u32[]{:S(2)}) %collective-permute-start) | collective-permute-done | bytes 131104 | tf_op jit(solution)/shard_map/ppermute | solution.py:509
  24.9 0.1 add_select_fusion.refs_0_
  25.0 0.5 %collective-permute-start.1 = (f32[32,1024]{1,0:T(8,128)S(1)}, f32[32,1024]{1,0:T(8,128)S(1)}, u32[]{:S(2)}, u32[]{:S(2)}) collective-permute-start(f32[32,1024]{1,0:T(8,128)S(1)} %add_select_fusion.refs_0_), channel_id=1, source_target_pairs={{0,24},{8,16},{16,8},{24,0},{1,25},{9,17},{17,9},{25,1},{2,26},{10... | collective-permute-start | bytes 393224 | tf_op jit(solution)/shard_map/ppermute | solution.py:509
  25.5 0.9 %collective-permute-start.2 = (f32[24,384]{1,0:T(8,128)S(1)}, f32[24,384]{1,0:T(8,128)S(1)}, u32[]{:S(2)}, u32[]{:S(2)}) collective-permute-start(f32[24,384]{1,0:T(8,128)S(1)} %get-tuple-element.21.refs_7_), channel_id=1, source_target_pairs={{0,1},{1,0},{2,3},{3,2},{4,5},{5,4},{6,7},{7,6},{8,9},{9,8},{10,11... | collective-permute-start | bytes 110600 | tf_op jit(solution)/shard_map/ppermute | solution.py:502
  26.4 3.8 %collective-permute-start.3 = (f32[24,384]{1,0:T(8,128)S(1)}, f32[24,384]{1,0:T(8,128)S(1)}, u32[]{:S(2)}, u32[]{:S(2)}) collective-permute-start(f32[24,384]{1,0:T(8,128)S(1)} %get-tuple-element.22.refs_8_), channel_id=1, source_target_pairs={{1,2},{2,1},{3,4},{4,3},{5,6},{6,5},{9,10},{10,9},{11,12},{12,11},... | collective-permute-start | bytes 110600 | tf_op jit(solution)/shard_map/ppermute | solution.py:503
  30.3 0.0 collective-permute-done.2.refs_9_
  30.3 2.9 %collective-permute-done.3.refs_10_ = f32[24,384]{1,0:T(8,128)S(1)} collective-permute-done((f32[24,384]{1,0:T(8,128)S(1)}, f32[24,384]{1,0:T(8,128)S(1)}, u32[]{:S(2)}, u32[]{:S(2)}) %collective-permute-start.3) | collective-permute-done | bytes 36896 | tf_op jit(solution)/shard_map/ppermute | solution.py:503
  33.2 0.0 collective-permute-done.1.refs_2_
  33.2 0.0 copy-done
  33.2 6.9 %nudge.1 = f32[24,384,128]{2,1,0:T(8,128)} custom-call(s32[8]{0:T(128)S(1)} %get-tuple-element.15.bounds_ref, f32[32,1024]{1,0:T(8,128)S(1)} %add_select_fusion.refs_0_, f32[32,1024]{1,0:T(8,128)S(1)} %collective-permute-done.refs_1_, f32[32,1024]{1,0:T(8,128)S(1)} %collective-permute-done.1.refs_2_, f32[24,1024]{1,0:T(8,128)S(1)} %get-tuple-element.17.refs_3_, ...), custom_call_target="tpu_custom_call" | custom-call | flops 4000000000 | bytes 10000000 | tf_op jit(solution)/shard_map/nudge/pallas_call | solution.py:514
  (1 shorter events, 0.0 us)
Async XLA Ops:
  2.2 13.0 %all-to-all-start = ((f32[32,8,128]{2,1,0:T(8,128)}), f32[32,8,128]{2,1,0:T(8,128)S(1)}, u32[]{:S(2)}, u32[]{:S(2)}) async-start(f32[32,8,128]{2,1,0:T(8,128)} %get-tuple-element.14), calls=%async_computation | async-start | bytes 262144 | tf_op jit(solution)/shard_map/all_to_all | solution.py:455
  15.2 17.9 %copy-start = (f32[24,24]{1,0:T(8,128)S(1)}, f32[24,24]{1,0:T(8,128)}, u32[]{:S(2)}) copy-start(f32[24,24]{1,0:T(8,128)} %get-tuple-element.18.refs_4_) | copy-start | bytes 6916
  23.5 1.4 %collective-permute-start = (f32[32,1024]{1,0:T(8,128)S(1)}, f32[32,1024]{1,0:T(8,128)S(1)}, u32[]{:S(2)}, u32[]{:S(2)}) collective-permute-start(f32[32,1024]{1,0:T(8,128)S(1)} %get-tuple-element.16), channel_id=1, source_target_pairs={{0,8},{8,0},{16,24},{24,16},{1,9},{9,1},{17,25},{25,17},{2,10},{10... | collective-permute-start | bytes 393224 | tf_op jit(solution)/shard_map/ppermute | solution.py:509
  25.0 8.2 %collective-permute-start.1 = (f32[32,1024]{1,0:T(8,128)S(1)}, f32[32,1024]{1,0:T(8,128)S(1)}, u32[]{:S(2)}, u32[]{:S(2)}) collective-permute-start(f32[32,1024]{1,0:T(8,128)S(1)} %add_select_fusion.refs_0_), channel_id=1, source_target_pairs={{0,24},{8,16},{16,8},{24,0},{1,25},{9,17},{17,9},{25,1},{2,26},{10... | collective-permute-start | bytes 393224 | tf_op jit(solution)/shard_map/ppermute | solution.py:509
  25.5 4.7 %collective-permute-start.2 = (f32[24,384]{1,0:T(8,128)S(1)}, f32[24,384]{1,0:T(8,128)S(1)}, u32[]{:S(2)}, u32[]{:S(2)}) collective-permute-start(f32[24,384]{1,0:T(8,128)S(1)} %get-tuple-element.21.refs_7_), channel_id=1, source_target_pairs={{0,1},{1,0},{2,3},{3,2},{4,5},{5,4},{6,7},{7,6},{8,9},{9,8},{10,11... | collective-permute-start | bytes 110600 | tf_op jit(solution)/shard_map/ppermute | solution.py:502
  26.4 6.7 %collective-permute-start.3 = (f32[24,384]{1,0:T(8,128)S(1)}, f32[24,384]{1,0:T(8,128)S(1)}, u32[]{:S(2)}, u32[]{:S(2)}) collective-permute-start(f32[24,384]{1,0:T(8,128)S(1)} %get-tuple-element.22.refs_8_), channel_id=1, source_target_pairs={{1,2},{2,1},{3,4},{4,3},{5,6},{6,5},{9,10},{10,9},{11,12},{12,11},... | collective-permute-start | bytes 110600 | tf_op jit(solution)/shard_map/ppermute | solution.py:503

commit v4 on v3

--- a/solution.py
+++ b/solution.py
@@ -84,7 +84,7 @@
     row = iota((8, records), 0)
     x_row = jnp.broadcast_to(x_ref[...].astype(jnp.float32), (8, records))
     y_row = jnp.broadcast_to(y_ref[...].astype(jnp.float32) - float(LANES), (8, records))
-    head = jnp.where(row == 0, x_row, jnp.where(row == 1, y_row, 0.0))
+    head = jnp.where(row % 4 == 0, x_row, jnp.where(row % 4 == 1, y_row, 0.0))
     payload = jnp.concatenate([head] + terms, axis=0)
 
     owner = owner_ref[...].astype(jnp.float32)
@@ -115,7 +115,7 @@
             inside = (lane >= LANE_STEP * j) & (lane < LANE_STEP * j + cap)
             block = jnp.where(inside, part, block)
         for g in range(msg_ref.shape[0] // count_y):
-            msg_ref[g * count_y + c] = block
+            msg_ref[g * count_y + c] = block[0:4] if g % 2 == 0 else block[4:8]
 
     gram = dot(vert, vert, NT, HIGHEST) * spread_gain
     alike = (iota((kinds, kinds), 0) // levels) == (iota((kinds, kinds), 1) // levels)
@@ -166,19 +166,21 @@
 ):
     kinds, tile_x, tile_y = state.shape
     width = cress.shape[0]
-    blocks = recv_ref.shape[0] * cap // RB
     cress_read = part_copies(cress_hbm, cress, cress_sems, width // PARTS)
     state_read = part_copies(state_hbm, state, state_sems, kinds // PARTS)
     each(PARTS, lambda i: cress_read(i).start())
     each(PARTS, lambda i: state_read(i).start())
-    slots = recv_ref.shape[0] * cap
+    slots = 2 * recv_ref.shape[0] * cap
+    blocks = slots // RB
     chunks = slots // LANES
 
     groups = [unpack(recv_ref, cap, j) for j in range(WORDS // 8)]
     keys = []
     for c in range(chunks):
         place = (iota((1, LANES), 1) + c * LANES).astype(jnp.float32)
-        keys.append((groups[0][c][1:2] + float(tile_y)) * float(slots) + place)
+        at = 1 if c < chunks // 2 else 5
+        y_row = groups[0][c % (chunks // 2)][at : at + 1]
+        keys.append((y_row + float(tile_y)) * float(slots) + place)
     counts = [jnp.zeros((8, LANES), jnp.float32) for _ in range(chunks)]
     for c in range(chunks):
         column = jnp.transpose(jnp.broadcast_to(keys[c], (LANES, LANES)))
@@ -188,7 +190,8 @@
     rank = jnp.concatenate([jnp.sum(count, axis=0, keepdims=True) for count in counts], axis=1)
 
     rows = []
-    head = jnp.concatenate(groups[0], axis=1)
+    pairs = [jnp.concatenate(group, axis=1) for group in groups]
+    head = jnp.concatenate([pairs[0], pltpu.roll(pairs[0], 4, 0)], axis=1)
     x_high = jnp.floor(head[0:1] * 0.0625)
     row = iota((8, slots), 0)
     top = jnp.where(
@@ -200,7 +203,14 @@
             jnp.where(row == 2, jnp.broadcast_to(head[1:2] + float(tile_y), (8, slots)), 0.0),
         ),
     )
-    words = jnp.concatenate([jnp.concatenate(group, axis=1) for group in groups[1:]], axis=0)
+    lower = iota((8, slots // 2), 0) < 4
+    words = jnp.concatenate(
+        [
+            jnp.concatenate([jnp.where(lower, pair, 0.0), jnp.where(lower, 0.0, pair)], axis=1)
+            for pair in pairs[1:]
+        ],
+        axis=0,
+    )
     high = words.astype(jnp.bfloat16).astype(jnp.float32)
     middle = (words - high).astype(jnp.bfloat16).astype(jnp.float32)
     low = words - high - middle
@@ -216,7 +226,11 @@
         x_rows.append(ordered[0:1] * 16.0 + ordered[1:2])
         ys = ordered[2:3]
         ys_ref[:, lanes] = jnp.broadcast_to(ys, (8, RB))
-        terms_ref[:, lanes] = ordered[8:32] + ordered[32:56] + ordered[56:80]
+        terms = ordered[8:32] + ordered[32:56] + ordered[56:80]
+        for v in range(3):
+            some = terms[8 * v : 8 * v + 8]
+            terms_ref[8 * v : 8 * v + 8, lanes] = some + pltpu.roll(some, 4, 0)
+        msg_ref[WORDS:, lanes] = terms_ref[:, lanes]
         least = jnp.min(ys).astype(jnp.int32)
         most = jnp.minimum(jnp.max(ys).astype(jnp.int32), tile_y - 1)
         bounds_ref[2 * j] = least // YB
@@ -271,7 +285,7 @@
         lanes = slice(j * RB, (j + 1) * RB)
         total = dot(ones, wt_ref[:, lanes])
         msg_ref[kinds : kinds + 1, lanes] = total[0:1]
-    msg_ref[kinds + 1 :, :] = jnp.zeros((WORDS - kinds - 1, slots), jnp.float32)
+    msg_ref[kinds + 1 : WORDS, :] = jnp.zeros((WORDS - kinds - 1, slots), jnp.float32)
     for side, edge in enumerate((0, tile_x - 1)):
         for k in range(kinds):
             msg_ref[edge_place(slots, k, side)] = state[k, edge : edge + 1, :]
@@ -335,7 +349,9 @@
     each(PARTS, lambda i: read(i).start())
     total = sum_ref[0 : kinds + 1, :] + recv_refs[-1][0 : kinds + 1, :]
     averaged = total[0:kinds] / total[kinds : kinds + 1]
-    spread_ref[0:kinds, :] = terms_ref[...] - dot(gram_ref[...], averaged, NN, HIGHEST)
+    upper = (iota(terms_ref.shape, 0) // (levels // 2)) % 2
+    terms = jnp.where(upper == lax.rem(me, 2), terms_ref[...], recv_refs[0][WORDS:, :])
+    spread_ref[0:kinds, :] = terms - dot(gram_ref[...], averaged, NN, HIGHEST)
     spread_ref[kinds : kinds + 1, :] = jnp.ones((1, slots), jnp.float32)
 
     y_blocks = tile_y // YB
@@ -433,7 +449,7 @@
     msg, gram = call(
         functools.partial(pack_kernel, count_y, cap),
         "pack_records",
-        (shape((count_x * count_y, 8, LANES), f32), shape((kinds, kinds), f32)),
+        (shape((count_x * count_y, 4, LANES), f32), shape((kinds, kinds), f32)),
         [HBM] * 5,
         (VMEM, VMEM),
         [pltpu.VMEM((1, records), i32)] * 3
@@ -453,6 +469,7 @@
         vertical.reshape(kinds, vertical.shape[2]),
     )
     recv = lax.all_to_all(msg, ("gx", "gy"), split_axis=0, concat_axis=0, tiled=True)
+    recv = recv.reshape(count_x * count_y // 2, 8, LANES)
 
     base = call(
         stencil_kernel,
@@ -475,7 +492,7 @@
         functools.partial(sums_kernel, cap),
         "column_sums",
         (
-            shape((WORDS, slots), f32),
+            shape((WORDS + kinds, slots), f32),
             shape((2 * tile_x, slots), bf16),
             shape((8, slots), f32),
             shape((kinds, slots), f32),
@@ -509,7 +526,7 @@
         got = lax.ppermute(summed, "gx", [(i, i ^ mask) for i in range(count_x)])
         received.append(got)
         if s < stages - 1:
-            summed = jnp.where(summing, summed + got, summed)
+            summed = jnp.where(summing, summed[:WORDS] + got[:WORDS], summed[:WORDS])
 
     out = call(
         functools.partial(nudge_kernel, stages),

time: 41.1 us -> 40.6 us (0.988); the launches traced: 40.3 us -> 40.4 us
    all_to_all x1, waiting for transfers between devices: 1.36 us -> 0.31 us  [local(): lax.all_to_all(msg, ('gx', 'gy'), split_axis=0, concat_axis=0, tiled=True)]
    ppermute x1, waiting for transfers between devices: 2.88 us -> 3.73 us  [local(): lax.ppermute(give_b, 'gy', [(i, (i - 1 ^ 1) + 1) for i in range(1, count_...]
    ppermute x1, starting transfers between devices: 3.84 us -> 2.99 us  [local(): lax.ppermute(give_b, 'gy', [(i, (i - 1 ^ 1) + 1) for i in range(1, count_...]
    ppermute x1, starting transfers between devices: 0.88 us -> 1.49 us  [local(): got_a = lax.ppermute(give_a, 'gy', [(i, i ^ 1) for i in range(count_y)])]
    ppermute x2, starting transfers between devices: 0.61 us -> 1.17 us  [local(): got = lax.ppermute(summed, 'gx', [(i, i ^ mask) for i in range(count_x)])]
where the time goes in v4:
time: 40.6 us; the launch traced here: 40.4 us
  Pallas kernels  23 us (57%)
  starting transfers between devices  11.7 us (29%)
  waiting for transfers between devices  5.42 us (13%)
    pallas_call x1, Pallas kernels, local(): call(functools.partial(sums_kernel, cap), 'column_sums', (shape((WORDS +...  8.27 us
    pallas_call x1, Pallas kernels, local(): call(functools.partial(nudge_kernel, stages), 'nudge', shape((kinds, tile...  6.96 us
    all_to_all x1, starting transfers between devices, local(): lax.all_to_all(msg, ('gx', 'gy'), split_axis=0, concat_axis=0, tiled=True)  6.05 us
    pallas_call x1, Pallas kernels, local(): call(stencil_kernel, 'stencil', shape(model_state.shape, f32), [HBM], HBM...  5.62 us
    ppermute x1, waiting for transfers between devices, local(): lax.ppermute(give_b, 'gy', [(i, (i - 1 ^ 1) + 1) for i in range(1, count_...  3.73 us
    ppermute x1, starting transfers between devices, local(): lax.ppermute(give_b, 'gy', [(i, (i - 1 ^ 1) + 1) for i in range(1, count_...  2.99 us
    pallas_call x1, Pallas kernels, local(): call(functools.partial(pack_kernel, count_y, cap), 'pack_records', (shape...  2.15 us
    ppermute x1, starting transfers between devices, local(): got_a = lax.ppermute(give_a, 'gy', [(i, i ^ 1) for i in range(count_y)])  1.49 us
  transfers between devices with their start and end apart: 5, of which 3 were waited for; matrix products, arithmetic and copies ran while one was open for 0% of the time, Pallas kernels for 14%

profile of v4, /device:TPU:8, one launch (start us, length us, event | category | flops | bytes accessed | tf_op | source)
XLA Modules:
  0.0 40.4 jit_solution(14204930049237495350)
XLA Ops:
  0.0 2.2 %pack_records.1 = (f32[32,4,128]{2,1,0:T(4,128)}, f32[24,24]{1,0:T(8,128)}) custom-call(s32[1,128]{1,0:T(1,128)} %bitcast.12, s32[1,128]{1,0:T(1,128)} %bitcast.13, s32[1,128]{1,0:T(1,128)} %bitcast.14, f32[128,384]{1,0:T(8,128)} %refs_3_.1, f32[24,128]{1,0:T(8,128)} %bitcast.11), custom_call_target="tpu_custom_call" | custom-call | flops 10000000 | bytes 1000000 | tf_op jit(solution)/shard_map/pack_records/pallas_call | solution.py:449
  2.2 6.0 %all-to-all-start = ((f32[32,4,128]{2,1,0:T(4,128)}), f32[32,4,128]{2,1,0:T(4,128)S(1)}, u32[]{:S(2)}, u32[]{:S(2)}) async-start(f32[32,4,128]{2,1,0:T(4,128)} %get-tuple-element.14), calls=%async_computation | async-start | bytes 131072 | tf_op jit(solution)/shard_map/all_to_all | solution.py:471
  8.2 5.6 %stencil.1.base_hbm = f32[3,8,384,128]{3,2,1,0:T(8,128)} custom-call(f32[3,8,384,128]{3,2,1,0:T(8,128)} %state_hbm.1), custom_call_target="tpu_custom_call" | custom-call | bytes 10000000 | tf_op jit(solution)/shard_map/stencil/pallas_call | solution.py:474
  13.8 0.3 all-to-all-done
  14.2 0.0 copy-start
  14.2 8.3 %column_sums.1 = (f32[56,1024]{1,0:T(8,128)S(1)}, bf16[768,1024]{1,0:T(8,128)(2,1)S(1)}, f32[8,1024]{1,0:T(8,128)S(1)}, f32[24,1024]{1,0:T(8,128)S(1)}, s32[8]{0...) custom-call(f32[16,8,128]{2,1,0:T(8,128)S(1)} %bitcast.8, f32[3,8,384,128]{3,2,1,0:T(8,128)} %stencil.1.base_hbm, ...), custom_call_target="tpu_custom_call" | custom-call | flops 4000000000 | bytes 10000000 | tf_op jit(solution)/shard_map/column_sums/pallas_call | solution.py:491
  22.4 0.2 collective-permute-start
  22.6 1.4 %collective-permute-done.refs_1_ = f32[56,1024]{1,0:T(8,128)S(1)} collective-permute-done((f32[56,1024]{1,0:T(8,128)S(1)}, f32[56,1024]{1,0:T(8,128)S(1)}, u32[]{:S(2)}, u32[]{:S(2)}) %collective-permute-start) | collective-permute-done | bytes 229408 | tf_op jit(solution)/shard_map/ppermute | solution.py:526
  24.0 0.1 add_select_fusion.refs_0_
  24.1 1.0 %collective-permute-start.1 = (f32[32,1024]{1,0:T(8,128)S(1)}, f32[32,1024]{1,0:T(8,128)S(1)}, u32[]{:S(2)}, u32[]{:S(2)}) collective-permute-start(f32[32,1024]{1,0:T(8,128)S(1)} %add_select_fusion.refs_0_), channel_id=1, source_target_pairs={{0,24},{8,16},{16,8},{24,0},{1,25},{9,17},{17,9},{25,1},{2,26},{10... | collective-permute-start | bytes 393224 | tf_op jit(solution)/shard_map/ppermute | solution.py:526
  25.1 1.5 %collective-permute-start.2 = (f32[24,384]{1,0:T(8,128)S(1)}, f32[24,384]{1,0:T(8,128)S(1)}, u32[]{:S(2)}, u32[]{:S(2)}) collective-permute-start(f32[24,384]{1,0:T(8,128)S(1)} %get-tuple-element.21.refs_7_), channel_id=1, source_target_pairs={{0,1},{1,0},{2,3},{3,2},{4,5},{5,4},{6,7},{7,6},{8,9},{9,8},{10,11... | collective-permute-start | bytes 110600 | tf_op jit(solution)/shard_map/ppermute | solution.py:519
  26.6 3.0 %collective-permute-start.3 = (f32[24,384]{1,0:T(8,128)S(1)}, f32[24,384]{1,0:T(8,128)S(1)}, u32[]{:S(2)}, u32[]{:S(2)}) collective-permute-start(f32[24,384]{1,0:T(8,128)S(1)} %get-tuple-element.22.refs_8_), channel_id=1, source_target_pairs={{1,2},{2,1},{3,4},{4,3},{5,6},{6,5},{9,10},{10,9},{11,12},{12,11},... | collective-permute-start | bytes 110600 | tf_op jit(solution)/shard_map/ppermute | solution.py:520
  29.6 0.0 collective-permute-done.2.refs_9_
  29.6 3.7 %collective-permute-done.3.refs_10_ = f32[24,384]{1,0:T(8,128)S(1)} collective-permute-done((f32[24,384]{1,0:T(8,128)S(1)}, f32[24,384]{1,0:T(8,128)S(1)}, u32[]{:S(2)}, u32[]{:S(2)}) %collective-permute-start.3) | collective-permute-done | bytes 36896 | tf_op jit(solution)/shard_map/ppermute | solution.py:520
  33.3 0.0 collective-permute-done.1.refs_2_
  33.3 0.0 copy-done
  33.3 7.0 %nudge.1 = f32[24,384,128]{2,1,0:T(8,128)} custom-call(s32[8]{0:T(128)S(1)} %get-tuple-element.15.bounds_ref, f32[32,1024]{1,0:T(8,128)S(1)} %add_select_fusion.refs_0_, f32[56,1024]{1,0:T(8,128)S(1)} %collective-permute-done.refs_1_, f32[32,1024]{1,0:T(8,128)S(1)} %collective-permute-done.1.refs_2_, f32[24,1024]{1,0:T(8,128)S(1)} %get-tuple-element.17.refs_3_, ...), custom_call_target="tpu_custom_call" | custom-call | flops 4000000000 | bytes 10000000 | tf_op jit(solution)/shard_map/nudge/pallas_call | solution.py:531
  (1 shorter events, 0.0 us)
Async XLA Ops:
  2.2 12.0 %all-to-all-start = ((f32[32,4,128]{2,1,0:T(4,128)}), f32[32,4,128]{2,1,0:T(4,128)S(1)}, u32[]{:S(2)}, u32[]{:S(2)}) async-start(f32[32,4,128]{2,1,0:T(4,128)} %get-tuple-element.14), calls=%async_computation | async-start | bytes 131072 | tf_op jit(solution)/shard_map/all_to_all | solution.py:471
  14.2 19.1 %copy-start = (f32[24,24]{1,0:T(8,128)S(1)}, f32[24,24]{1,0:T(8,128)}, u32[]{:S(2)}) copy-start(f32[24,24]{1,0:T(8,128)} %get-tuple-element.18.refs_4_) | copy-start | bytes 6916
  22.4 1.6 %collective-permute-start = (f32[56,1024]{1,0:T(8,128)S(1)}, f32[56,1024]{1,0:T(8,128)S(1)}, u32[]{:S(2)}, u32[]{:S(2)}) collective-permute-start(f32[56,1024]{1,0:T(8,128)S(1)} %get-tuple-element.16), channel_id=1, source_target_pairs={{0,8},{8,0},{16,24},{24,16},{1,9},{9,1},{17,25},{25,17},{2,10},{10... | collective-permute-start | bytes 688136 | tf_op jit(solution)/shard_map/ppermute | solution.py:526
  24.1 9.2 %collective-permute-start.1 = (f32[32,1024]{1,0:T(8,128)S(1)}, f32[32,1024]{1,0:T(8,128)S(1)}, u32[]{:S(2)}, u32[]{:S(2)}) collective-permute-start(f32[32,1024]{1,0:T(8,128)S(1)} %add_select_fusion.refs_0_), channel_id=1, source_target_pairs={{0,24},{8,16},{16,8},{24,0},{1,25},{9,17},{17,9},{25,1},{2,26},{10... | collective-permute-start | bytes 393224 | tf_op jit(solution)/shard_map/ppermute | solution.py:526
  25.1 4.5 %collective-permute-start.2 = (f32[24,384]{1,0:T(8,128)S(1)}, f32[24,384]{1,0:T(8,128)S(1)}, u32[]{:S(2)}, u32[]{:S(2)}) collective-permute-start(f32[24,384]{1,0:T(8,128)S(1)} %get-tuple-element.21.refs_7_), channel_id=1, source_target_pairs={{0,1},{1,0},{2,3},{3,2},{4,5},{5,4},{6,7},{7,6},{8,9},{9,8},{10,11... | collective-permute-start | bytes 110600 | tf_op jit(solution)/shard_map/ppermute | solution.py:519
  26.6 6.7 %collective-permute-start.3 = (f32[24,384]{1,0:T(8,128)S(1)}, f32[24,384]{1,0:T(8,128)S(1)}, u32[]{:S(2)}, u32[]{:S(2)}) collective-permute-start(f32[24,384]{1,0:T(8,128)S(1)} %get-tuple-element.22.refs_8_), channel_id=1, source_target_pairs={{1,2},{2,1},{3,4},{4,3},{5,6},{6,5},{9,10},{10,9},{11,12},{12,11},... | collective-permute-start | bytes 110600 | tf_op jit(solution)/shard_map/ppermute | solution.py:520

commit v5 on v4

--- a/solution.py
+++ b/solution.py
@@ -247,6 +247,7 @@
         hot = jnp.where(iota((width, RB), 0).astype(jnp.float32) == x_rows[j], 1.0, 0.0)
         wt = dot(ct[...], hot.astype(jnp.bfloat16))
         wt_ref[:, j * RB : (j + 1) * RB] = wt.astype(jnp.bfloat16)
+        msg_ref[kinds : kinds + 1, j * RB : (j + 1) * RB] = jnp.sum(wt, axis=0, keepdims=True)
 
     half = blocks // 2
     for j in range(half):
@@ -280,11 +281,6 @@
         before = j
         msg_ref[0:kinds, lanes] = running
 
-    ones = jnp.ones((8, 2 * tile_x), jnp.bfloat16)
-    for j in range(blocks):
-        lanes = slice(j * RB, (j + 1) * RB)
-        total = dot(ones, wt_ref[:, lanes])
-        msg_ref[kinds : kinds + 1, lanes] = total[0:1]
     msg_ref[kinds + 1 : WORDS, :] = jnp.zeros((WORDS - kinds - 1, slots), jnp.float32)
     for side, edge in enumerate((0, tile_x - 1)):
         for k in range(kinds):

time: 40.6 us -> 40.6 us (level)
  no operation moved by 1% of the time
where the time goes in v5:
time: 40.6 us; the launch traced here: 40.4 us
  Pallas kernels  23 us (57%)
  starting transfers between devices  11.7 us (29%)
  waiting for transfers between devices  5.41 us (13%)
    pallas_call x1, Pallas kernels, local(): call(functools.partial(sums_kernel, cap), 'column_sums', (shape((WORDS +...  8.27 us
    pallas_call x1, Pallas kernels, local(): call(functools.partial(nudge_kernel, stages), 'nudge', shape((kinds, tile...  6.92 us
    all_to_all x1, starting transfers between devices, local(): lax.all_to_all(msg, ('gx', 'gy'), split_axis=0, concat_axis=0, tiled=True)  6.05 us
    pallas_call x1, Pallas kernels, local(): call(stencil_kernel, 'stencil', shape(model_state.shape, f32), [HBM], HBM...  5.62 us
    ppermute x1, waiting for transfers between devices, local(): lax.ppermute(give_b, 'gy', [(i, (i - 1 ^ 1) + 1) for i in range(1, count_...  3.73 us
    ppermute x1, starting transfers between devices, local(): lax.ppermute(give_b, 'gy', [(i, (i - 1 ^ 1) + 1) for i in range(1, count_...  2.99 us
    pallas_call x1, Pallas kernels, local(): call(functools.partial(pack_kernel, count_y, cap), 'pack_records', (shape...  2.15 us
    ppermute x1, starting transfers between devices, local(): got_a = lax.ppermute(give_a, 'gy', [(i, i ^ 1) for i in range(count_y)])  1.5 us
  transfers between devices with their start and end apart: 5, of which 3 were waited for; matrix products, arithmetic and copies ran while one was open for 0% of the time, Pallas kernels for 14%

profile of v5, /device:TPU:8, one launch (start us, length us, event | category | flops | bytes accessed | tf_op | source)
XLA Modules:
  0.0 40.4 jit_solution(16582499889330915600)
XLA Ops:
  0.0 2.2 %pack_records.1 = (f32[32,4,128]{2,1,0:T(4,128)}, f32[24,24]{1,0:T(8,128)}) custom-call(s32[1,128]{1,0:T(1,128)} %bitcast.12, s32[1,128]{1,0:T(1,128)} %bitcast.13, s32[1,128]{1,0:T(1,128)} %bitcast.14, f32[128,384]{1,0:T(8,128)} %refs_3_.1, f32[24,128]{1,0:T(8,128)} %bitcast.11), custom_call_target="tpu_custom_call" | custom-call | flops 10000000 | bytes 1000000 | tf_op jit(solution)/shard_map/pack_records/pallas_call | solution.py:445
  2.2 6.0 %all-to-all-start = ((f32[32,4,128]{2,1,0:T(4,128)}), f32[32,4,128]{2,1,0:T(4,128)S(1)}, u32[]{:S(2)}, u32[]{:S(2)}) async-start(f32[32,4,128]{2,1,0:T(4,128)} %get-tuple-element.14), calls=%async_computation | async-start | bytes 131072 | tf_op jit(solution)/shard_map/all_to_all | solution.py:467
  8.2 5.6 %stencil.1.base_hbm = f32[3,8,384,128]{3,2,1,0:T(8,128)} custom-call(f32[3,8,384,128]{3,2,1,0:T(8,128)} %state_hbm.1), custom_call_target="tpu_custom_call" | custom-call | bytes 10000000 | tf_op jit(solution)/shard_map/stencil/pallas_call | solution.py:470
  13.8 0.3 all-to-all-done
  14.2 0.0 copy-start
  14.2 8.3 %column_sums.1 = (f32[56,1024]{1,0:T(8,128)S(1)}, bf16[768,1024]{1,0:T(8,128)(2,1)S(1)}, f32[8,1024]{1,0:T(8,128)S(1)}, f32[24,1024]{1,0:T(8,128)S(1)}, s32[8]{0...) custom-call(f32[16,8,128]{2,1,0:T(8,128)S(1)} %bitcast.8, f32[3,8,384,128]{3,2,1,0:T(8,128)} %stencil.1.base_hbm, ...), custom_call_target="tpu_custom_call" | custom-call | flops 4000000000 | bytes 10000000 | tf_op jit(solution)/shard_map/column_sums/pallas_call | solution.py:487
  22.4 0.2 collective-permute-start
  22.6 1.4 %collective-permute-done.refs_1_ = f32[56,1024]{1,0:T(8,128)S(1)} collective-permute-done((f32[56,1024]{1,0:T(8,128)S(1)}, f32[56,1024]{1,0:T(8,128)S(1)}, u32[]{:S(2)}, u32[]{:S(2)}) %collective-permute-start) | collective-permute-done | bytes 229408 | tf_op jit(solution)/shard_map/ppermute | solution.py:522
  24.0 0.1 add_select_fusion.refs_0_
  24.1 1.0 %collective-permute-start.1 = (f32[32,1024]{1,0:T(8,128)S(1)}, f32[32,1024]{1,0:T(8,128)S(1)}, u32[]{:S(2)}, u32[]{:S(2)}) collective-permute-start(f32[32,1024]{1,0:T(8,128)S(1)} %add_select_fusion.refs_0_), channel_id=1, source_target_pairs={{0,24},{8,16},{16,8},{24,0},{1,25},{9,17},{17,9},{25,1},{2,26},{10... | collective-permute-start | bytes 393224 | tf_op jit(solution)/shard_map/ppermute | solution.py:522
  25.1 1.5 %collective-permute-start.2 = (f32[24,384]{1,0:T(8,128)S(1)}, f32[24,384]{1,0:T(8,128)S(1)}, u32[]{:S(2)}, u32[]{:S(2)}) collective-permute-start(f32[24,384]{1,0:T(8,128)S(1)} %get-tuple-element.21.refs_7_), channel_id=1, source_target_pairs={{0,1},{1,0},{2,3},{3,2},{4,5},{5,4},{6,7},{7,6},{8,9},{9,8},{10,11... | collective-permute-start | bytes 110600 | tf_op jit(solution)/shard_map/ppermute | solution.py:515
  26.6 3.0 %collective-permute-start.3 = (f32[24,384]{1,0:T(8,128)S(1)}, f32[24,384]{1,0:T(8,128)S(1)}, u32[]{:S(2)}, u32[]{:S(2)}) collective-permute-start(f32[24,384]{1,0:T(8,128)S(1)} %get-tuple-element.22.refs_8_), channel_id=1, source_target_pairs={{1,2},{2,1},{3,4},{4,3},{5,6},{6,5},{9,10},{10,9},{11,12},{12,11},... | collective-permute-start | bytes 110600 | tf_op jit(solution)/shard_map/ppermute | solution.py:516
  29.6 0.0 collective-permute-done.2.refs_9_
  29.6 3.7 %collective-permute-done.3.refs_10_ = f32[24,384]{1,0:T(8,128)S(1)} collective-permute-done((f32[24,384]{1,0:T(8,128)S(1)}, f32[24,384]{1,0:T(8,128)S(1)}, u32[]{:S(2)}, u32[]{:S(2)}) %collective-permute-start.3) | collective-permute-done | bytes 36896 | tf_op jit(solution)/shard_map/ppermute | solution.py:516
  33.3 0.0 collective-permute-done.1.refs_2_
  33.3 0.0 copy-done
  33.3 6.9 %nudge.1 = f32[24,384,128]{2,1,0:T(8,128)} custom-call(s32[8]{0:T(128)S(1)} %get-tuple-element.15.bounds_ref, f32[32,1024]{1,0:T(8,128)S(1)} %add_select_fusion.refs_0_, f32[56,1024]{1,0:T(8,128)S(1)} %collective-permute-done.refs_1_, f32[32,1024]{1,0:T(8,128)S(1)} %collective-permute-done.1.refs_2_, f32[24,1024]{1,0:T(8,128)S(1)} %get-tuple-element.17.refs_3_, ...), custom_call_target="tpu_custom_call" | custom-call | flops 4000000000 | bytes 10000000 | tf_op jit(solution)/shard_map/nudge/pallas_call | solution.py:527
  (1 shorter events, 0.0 us)
Async XLA Ops:
  2.2 12.0 %all-to-all-start = ((f32[32,4,128]{2,1,0:T(4,128)}), f32[32,4,128]{2,1,0:T(4,128)S(1)}, u32[]{:S(2)}, u32[]{:S(2)}) async-start(f32[32,4,128]{2,1,0:T(4,128)} %get-tuple-element.14), calls=%async_computation | async-start | bytes 131072 | tf_op jit(solution)/shard_map/all_to_all | solution.py:467
  14.2 19.2 %copy-start = (f32[24,24]{1,0:T(8,128)S(1)}, f32[24,24]{1,0:T(8,128)}, u32[]{:S(2)}) copy-start(f32[24,24]{1,0:T(8,128)} %get-tuple-element.18.refs_4_) | copy-start | bytes 6916
  22.4 1.6 %collective-permute-start = (f32[56,1024]{1,0:T(8,128)S(1)}, f32[56,1024]{1,0:T(8,128)S(1)}, u32[]{:S(2)}, u32[]{:S(2)}) collective-permute-start(f32[56,1024]{1,0:T(8,128)S(1)} %get-tuple-element.16), channel_id=1, source_target_pairs={{0,8},{8,0},{16,24},{24,16},{1,9},{9,1},{17,25},{25,17},{2,10},{10... | collective-permute-start | bytes 688136 | tf_op jit(solution)/shard_map/ppermute | solution.py:522
  24.1 9.2 %collective-permute-start.1 = (f32[32,1024]{1,0:T(8,128)S(1)}, f32[32,1024]{1,0:T(8,128)S(1)}, u32[]{:S(2)}, u32[]{:S(2)}) collective-permute-start(f32[32,1024]{1,0:T(8,128)S(1)} %add_select_fusion.refs_0_), channel_id=1, source_target_pairs={{0,24},{8,16},{16,8},{24,0},{1,25},{9,17},{17,9},{25,1},{2,26},{10... | collective-permute-start | bytes 393224 | tf_op jit(solution)/shard_map/ppermute | solution.py:522
  25.1 4.5 %collective-permute-start.2 = (f32[24,384]{1,0:T(8,128)S(1)}, f32[24,384]{1,0:T(8,128)S(1)}, u32[]{:S(2)}, u32[]{:S(2)}) collective-permute-start(f32[24,384]{1,0:T(8,128)S(1)} %get-tuple-element.21.refs_7_), channel_id=1, source_target_pairs={{0,1},{1,0},{2,3},{3,2},{4,5},{5,4},{6,7},{7,6},{8,9},{9,8},{10,11... | collective-permute-start | bytes 110600 | tf_op jit(solution)/shard_map/ppermute | solution.py:515
  26.6 6.7 %collective-permute-start.3 = (f32[24,384]{1,0:T(8,128)S(1)}, f32[24,384]{1,0:T(8,128)S(1)}, u32[]{:S(2)}, u32[]{:S(2)}) collective-permute-start(f32[24,384]{1,0:T(8,128)S(1)} %get-tuple-element.22.refs_8_), channel_id=1, source_target_pairs={{1,2},{2,1},{3,4},{4,3},{5,6},{6,5},{9,10},{10,9},{11,12},{12,11},... | collective-permute-start | bytes 110600 | tf_op jit(solution)/shard_map/ppermute | solution.py:516
